TPU v7x, 256 devices: a whole 4x4x8 slice. The times are simulated.
256 devices in a mesh: grp: 8 (over x_hi, y), col: 32 (over z, x_lo, core).
Axes of the slice: x: 4 (x_hi: 2, x_lo: 2; x = x_hi * 2 + x_lo), y: 4, z: 8, core: 2. Of those that a mesh axis runs over, the one named last changes fastest.
Arguments:
- image_learn: bfloat16 [16384, 1152], P(('grp', 'col')), may hold values from -6 to 6
- image_refer: bfloat16 [16384, 1152], P(('grp', 'col')), may hold values from -6 to 6
- text_learn: bfloat16 [32, 1536, 1152], P('col', 'grp'), may hold values from -6 to 6
- text_refer: bfloat16 [32, 1536, 1152], P('col', 'grp'), may hold values from -6 to 6
- image_scale_learn: float32 [16384], P('grp'), may hold values from 0.03432945 to 0.102988355
- image_scale_refer: float32 [16384], P('grp'), may hold values from 0.03432945 to 0.102988355
- text_scale_learn: float32 [49152], P('col'), may hold values from 0.03432945 to 0.102988355
- text_scale_refer: float32 [49152], P('col'), may hold values from 0.03432945 to 0.102988355
- pair_index: int32 [16384], P('grp'), may hold values from 0 to 49151
Outputs:
- row_sum: float32 [16384], P(('grp', 'col'))
- col_sum: float32 [49152], P('col')
All inputs are finite; a program needn't handle non-finite values.
Results may differ from a plain program's by a relative error of at most 0.0003.
Values may be sent and summed in bfloat16 or wider, within the bound.
A program may use at most 128 MiB of HBM per device.

v0:
```python
import math

import jax
import jax.numpy as jnp
from jax import lax
from jax.sharding import PartitionSpec as P


def pair_score(learn_sim, refer_sim, positive, offset):
    sign = jnp.where(positive, jnp.float32(1.0), jnp.float32(-1.0))
    first = jax.nn.softplus(-sign * (4.0 * learn_sim + 1.0 - offset))
    second = jax.nn.softplus(-sign * (6.0 * refer_sim - 1.0 - offset))
    return first - second


def inner(left, right):
    return lax.dot_general(
        left, right, (((1,), (1,)), ((), ())), preferred_element_type=jnp.float32
    )


def shards(
    image_learn,
    image_refer,
    text_learn,
    text_refer,
    image_scale_learn,
    image_scale_refer,
    text_scale_learn,
    text_scale_refer,
    pair_index,
):
    texts = (
        lax.all_gather(text_learn, "grp", axis=1, tiled=True),
        lax.all_gather(text_refer, "grp", axis=1, tiled=True),
    )
    text_rows_learn = texts[0][0]
    text_rows_refer = texts[1][0]
    width = text_rows_learn.shape[0]
    offset = math.log(width * lax.axis_size("col"))
    columns = lax.axis_index("col") * width + jnp.arange(width, dtype=jnp.int32)
    images = (
        lax.all_gather(image_learn, "col", axis=0, tiled=True),
        lax.all_gather(image_refer, "col", axis=0, tiled=True),
    )
    learn_sim = (
        inner(images[0], text_rows_learn) * image_scale_learn[:, None] * text_scale_learn[None, :]
    )
    refer_sim = (
        inner(images[1], text_rows_refer) * image_scale_refer[:, None] * text_scale_refer[None, :]
    )
    learned = pair_score(learn_sim, refer_sim, pair_index[:, None] == columns[None, :], offset)
    row_part = lax.psum_scatter(jnp.sum(learned, axis=1), "col", scatter_dimension=0, tiled=True)
    col_local = jnp.sum(learned, axis=0)
    col_part = lax.psum(col_local, "grp")
    return (row_part, col_part)


def solution(mesh):
    in_specs = (
        P(("grp", "col"), None),
        P(("grp", "col"), None),
        P("col", "grp", None),
        P("col", "grp", None),
        P("grp"),
        P("grp"),
        P("col"),
        P("col"),
        P("grp"),
    )
    out_specs = (P(("grp", "col")), P("col"))
    return jax.shard_map(shards, mesh=mesh, in_specs=in_specs, out_specs=out_specs, check_vma=False)
```

profile of v0, /device:TPU:1, one launch (start us, length us, event | category | flops | bytes accessed | tf_op | source)
XLA Modules:
  0.0 404.1 jit_solution(7720731369672136523)
XLA Ops:
  7.2 0.0 all-gather.7.cloned.1.call-start
  7.2 0.7 all-gather.7.cloned.1.call-update
  7.9 0.0 all-gather.5.cloned.1.call-start
  7.9 0.7 all-gather.5.cloned.1.call-update
  8.6 0.0 all-gather.11.cloned.1.call-start
  8.7 0.7 all-gather.11.cloned.1.call-update
  9.4 0.0 all-gather.9.cloned.1.call-start
  9.4 0.5 all-gather.9.cloned.1.call-update
  10.0 1.3 dynamic-slice
  11.9 0.0 copy-start
  11.9 0.0 copy-start.1
  11.9 0.0 copy-start.2
  11.9 0.0 copy-start.3
  11.9 0.0 copy-start.4
  12.0 73.0 %all-gather.7.cloned.1.call-done = bf16[1,1536,1152]{2,1,0:T(8,128)(2,1)} async-done(((bf16[1,192,1152]{2,1,0:T(8,128)(2,1)}), bf16[1,1536,1152]{2,1,0:T(8,128)(2,1)}) %all-gather.7.cloned.1.call-update) | async-done | bytes 3538960 | tf_op jit(solution)/shard_map/all_gather | solution.py:34
  85.0 68.6 %all-gather.5.cloned.1.call-done = bf16[2048,1152]{1,0:T(8,128)(2,1)} async-done(((bf16[64,1152]{1,0:T(8,128)(2,1)}), bf16[2048,1152]{1,0:T(8,128)(2,1)}) %all-gather.5.cloned.1.call-update) | async-done | bytes 4718608 | tf_op jit(solution)/shard_map/all_gather | solution.py:43
  153.6 14.2 %fusion.2 = f32[2048,1536]{1,0:T(8,128)} fusion(bf16[2048,1152]{1,0:T(8,128)(2,1)} %all-gather.5.cloned.1.call-done, bf16[1,1536,1152]{2,1,0:T(8,128)(2,1)} %all-gather.7.cloned.1.call-done), kind=kOutput, calls=%fused_computation.4 | convolution fusion | flops 7247757312 | bytes 20840448 | tf_op jit(solution)/shard_map/dot_general | solution.py:17
  167.9 58.0 %all-gather.11.cloned.1.call-done = bf16[1,1536,1152]{2,1,0:T(8,128)(2,1)} async-done(((bf16[1,192,1152]{2,1,0:T(8,128)(2,1)}), bf16[1,1536,1152]{2,1,0:T(8,128)(2,1)}) %all-gather.11.cloned.1.call-update) | async-done | bytes 3538960 | tf_op jit(solution)/shard_map/all_gather | solution.py:35
  225.9 68.5 %all-gather.9.cloned.1.call-done = bf16[2048,1152]{1,0:T(8,128)(2,1)} async-done(((bf16[64,1152]{1,0:T(8,128)(2,1)}), bf16[2048,1152]{1,0:T(8,128)(2,1)}) %all-gather.9.cloned.1.call-update) | async-done | bytes 4718608 | tf_op jit(solution)/shard_map/all_gather | solution.py:44
  294.4 0.0 copy-done
  294.4 0.0 copy-done.1
  294.4 0.0 copy-done.2
  294.4 0.0 copy-done.3
  294.4 0.0 copy-done.4
  294.4 28.1 %fusion.4 = (f32[1536]{0:T(1024)S(1)}, f32[2048]{0:T(1024)S(1)}) fusion(f32[1536]{0:T(1024)S(1)} %copy-done, f32[2048]{0:T(1024)S(1)} %copy-done.1, bf16[2048,1152]{1,0:T(8,128)(2,1)} %all-gather.9.cloned.1.call-done, bf16[1,1536,1152]{2,1,0:T(8,128)(2,1)} %all-gather.11.cloned.1.call-done, f32[1536]{0:T(1024)S(1)} %copy-done.2, f32[2048,1536]{1,0:T(8,128)} %fusion.2, ...), kind=kOutput, calls=%fused_computation.7 | convolution fusion | flops 7335834112 | bytes 20897792 | tf_op jit(solution)/shard_map/dot_general | solution.py:17
  322.5 53.6 %all-reduce = f32[2048]{0:T(1024)S(1)} all-reduce(f32[2048]{0:T(1024)S(1)} %get-tuple-element.3), channel_id=2, replica_groups=mesh['grp'=8,'col'=32] {'col'}, use_global_device_ids=true, to_apply=%region_1.2.clone | all-reduce | flops 2048 | bytes 16384
  376.1 20.9 %psum.7 = f32[1536]{0:T(1024)} all-reduce(f32[1536]{0:T(1024)S(1)} %get-tuple-element.2), channel_id=1, replica_groups=mesh['grp'=8,'col'=32] {'grp'}, use_global_device_ids=true, to_apply=%region_3.4 | all-reduce | flops 1536 | bytes 12288 | tf_op jit(solution)/shard_map/psum | solution.py:55
  397.0 0.6 dynamic-slice.1
  (1 shorter events, 0.0 us)
Async XLA Ops:
  7.2 77.8 %all-gather.7.cloned.1.call-start = ((), (), s32[]{:S(2)}) async-start(), calls=%async_computation.1 | async-start | bytes 3981312 | tf_op jit(solution)/shard_map/all_gather | solution.py:34
  7.9 145.7 %all-gather.5.cloned.1.call-start = ((), (), s32[]{:S(2)}) async-start(), calls=%async_computation | async-start | bytes 4866048 | tf_op jit(solution)/shard_map/all_gather | solution.py:43
  8.6 217.2 %all-gather.11.cloned.1.call-start = ((), (), s32[]{:S(2)}) async-start(), calls=%async_computation.3 | async-start | bytes 3981312 | tf_op jit(solution)/shard_map/all_gather | solution.py:35
  9.4 285.0 %all-gather.9.cloned.1.call-start = ((), (), s32[]{:S(2)}) async-start(), calls=%async_computation.2 | async-start | bytes 4866048 | tf_op jit(solution)/shard_map/all_gather | solution.py:44
  11.9 282.5 %copy-start = (f32[1536]{0:T(1024)S(1)}, f32[1536]{0:T(1024)}, u32[]{:S(2)}) copy-start(f32[1536]{0:T(1024)} %param.16) | copy-start | bytes 18436
  11.9 282.5 %copy-start.1 = (f32[2048]{0:T(1024)S(1)}, f32[2048]{0:T(1024)}, u32[]{:S(2)}) copy-start(f32[2048]{0:T(1024)} %param.14) | copy-start | bytes 24580
  11.9 282.4 %copy-start.2 = (f32[1536]{0:T(1024)S(1)}, f32[1536]{0:T(1024)}, u32[]{:S(2)}) copy-start(f32[1536]{0:T(1024)} %param.15) | copy-start | bytes 18436
  11.9 282.4 %copy-start.3 = (f32[2048]{0:T(1024)S(1)}, f32[2048]{0:T(1024)}, u32[]{:S(2)}) copy-start(f32[2048]{0:T(1024)} %param.13) | copy-start | bytes 24580
  11.9 282.4 %copy-start.4 = (s32[2048]{0:T(1024)S(1)}, s32[2048]{0:T(1024)}, u32[]{:S(2)}) copy-start(s32[2048]{0:T(1024)} %param.17) | copy-start | bytes 24580
Sparse Core Ops, SparseCore 0:
  10.6 74.3 all-gather.6
  86.9 66.7 all-gather.4
  156.2 69.6 all-gather.10
  227.6 66.7 all-gather.8
where the time goes:
time: 407 us; the launch traced here: 404 us
  waiting for transfers between devices  271 us (67%)
  blocking collectives  74.5 us (18%)
  matrix products  42.3 us (10%)
  between operations  14.5 us (4%)
    all_gather x1, waiting for transfers between devices, shards(): lax.all_gather(text_learn, 'grp', axis=1, tiled=True)  73 us
    all_gather x1, waiting for transfers between devices, shards(): lax.all_gather(image_learn, 'col', axis=0, tiled=True)  68.6 us
    all_gather x1, waiting for transfers between devices, shards(): lax.all_gather(image_refer, 'col', axis=0, tiled=True)  68.5 us
    all_gather x1, waiting for transfers between devices, shards(): lax.all_gather(text_refer, 'grp', axis=1, tiled=True)  58 us
    unnamed x1, blocking collectives  53.6 us
    dot_general x2, matrix products, inner(): lax.dot_general(left, right, (((1,), (1,)), ((), ())), preferred_element_...  42.3 us
    psum x1, blocking collectives, shards(): col_part = lax.psum(col_local, 'grp')  20.9 us
  transfers between devices with their start and end apart: 4, of which 4 were waited for; matrix products, arithmetic and copies ran while one was open for 4% of the time, Pallas kernels for 0%

commit v1 on v0

v1 whole, which is shorter than its diff:
```python
import functools
import math

import jax
import jax.numpy as jnp
from jax import lax
from jax.experimental import pallas as pl
from jax.experimental.pallas import tpu as pltpu
from jax.sharding import PartitionSpec as P

F32 = jnp.float32
LOG2E = 1.0 / math.log(2.0)
LN2 = math.log(2.0)
SERIES = tuple(2.0 * LOG2E * c for c in (0.99999984, 0.33337989, 0.1979503, 0.17111227))

E = 1152
HALF = 96
CHUNK = 4 * HALF
SLOT = 256
SLOT_Z = (0, 1, -1, 2, -2, 3, -3, 4)
STEPS = 32


def wrap(value, size):
    return lax.rem(value + size, size)


def score(dot_learn, dot_refer, a_learn, a_refer, b_learn, b_refer, paired, c_learn, c_refer):
    u = dot_learn * a_learn * b_learn + c_learn
    w = dot_refer * a_refer * b_refer + c_refer
    p = jnp.exp2(-jnp.abs(u))
    q = jnp.exp2(-jnp.abs(w))
    z = (p - q) * pl.reciprocal((p + q) + 2.0, approx=True)
    s = z * z
    poly = s * SERIES[3] + SERIES[2]
    poly = poly * s + SERIES[1]
    poly = poly * s + SERIES[0]
    d = (jnp.maximum(u, 0.0) - jnp.maximum(w, 0.0)) + z * poly
    return d - jnp.where(paired, u - w, 0.0)


def kernel(
    c_learn,
    c_refer,
    img_l,
    img_r,
    txt_l,
    txt_r,
    isc_l,
    isc_r,
    tsc_l,
    tsc_r,
    pair,
    row_out,
    col_out,
    tb,
    ib,
    isc,
    ipr,
    tsc,
    bc,
    tcol,
    irow,
    iprow,
    base,
    rs,
    cs,
    dl0,
    dr0,
    dl1,
    dr1,
    row_part,
    row_recv,
    col_part,
    col_recv,
    local_sem,
    send_sem,
    recv_sem,
    row_send,
    row_got,
    col_send,
    col_got,
    ready,
):
    grp, col = lax.axis_index("grp"), lax.axis_index("col")
    x = lax.div(grp, 4) * 2 + lax.rem(lax.div(col, 2), 2)
    y = lax.rem(grp, 4)
    z = lax.div(col, 4)
    core = lax.rem(col, 2)
    x_odd, y_odd = lax.rem(x, 2), lax.rem(y, 2)
    x_pair, y_pair = x + 1 - 2 * x_odd, y + 1 - 2 * y_odd
    x_diag, y_diag = wrap(x - 1 + 2 * x_odd, 4), wrap(y - 1 + 2 * y_odd, 4)

    def device(dx=0, dy=0, dz=0, at_x=None, at_y=None, at_core=None):
        px = wrap(x + dx, 4) if at_x is None else at_x
        py = wrap(y + dy, 4) if at_y is None else at_y
        pz = wrap(z + dz, 8)
        pc = core if at_core is None else at_core
        return lax.div(px, 2) * 4 + py, (pz * 2 + lax.rem(px, 2)) * 2 + pc

    other_core = device(at_core=1 - core)
    diag = device(at_x=x_diag, at_y=y_diag)
    to_x_pair, to_y_pair = device(at_x=x_pair), device(at_y=y_pair)
    up_x, dn_x = device(dx=1), device(dx=-1)
    up_y, dn_y = device(dy=1), device(dy=-1)
    up_z, dn_z = device(dz=1), device(dz=-1)

    messages = {}

    def message(name, src, dst, to):
        messages[name] = (len(messages), src, dst, to)

    def text(piece, part=None):
        off, rows = (piece * HALF, HALF) if part is None else (piece * HALF + part * (HALF // 2), HALF // 2)
        return tb.at[:, pl.ds(off, rows), :]

    def image(slot, lane, part=None):
        rows = 64 if part is None else 32
        off = slot * SLOT + lane * 128 + core * 64 + (0 if part is None else part * 32)
        return ib.at[:, pl.ds(pl.multiple_of(off, 32), rows), :]

    message("t1p", text(0), text(2), to_x_pair)
    message("t2p", text(1), text(3), to_y_pair)
    message("ip", image(0, 0), image(0, 1), diag)
    message("tsc", tsc.at[0], tsc.at[1], to_x_pair)
    message("isc", isc.at[0], isc.at[1], diag)
    message("ipr", ipr.at[0], ipr.at[1], diag)
    for name, first, up, dn in (("t1", 0, up_y, dn_y), ("t2", 1, up_x, dn_x)):
        o = 4 + 2 * first
        message(name + "o-", text(first), text(o + 1), up)
        message(name + "o+", text(first), text(o), dn)
        message(name + "q-", text(2 + first), text(o + 5), up)
        message(name + "q+", text(2 + first), text(o + 4), dn)
        far = 12 + 2 * first
        message(name + "o2+", text(o, 0), text(far, 0), dn)
        message(name + "o2-", text(o + 1, 1), text(far, 1), up)
        message(name + "q2+", text(o + 4, 0), text(far + 1, 0), dn)
        message(name + "q2-", text(o + 5, 1), text(far + 1, 1), up)
    for lane, mark in ((0, "o"), (1, "q")):
        for k in (1, 2, 3):
            came_p, came_m = (0, 0) if k == 1 else (2 * k - 3, 2 * k - 2)
            message(f"i{mark}{k}+", image(came_p, lane), image(2 * k - 1, lane), dn_z)
            message(f"i{mark}{k}-", image(came_m, lane), image(2 * k, lane), up_z)
        message(f"i{mark}4+", image(5, lane, 0), image(7, lane, 0), dn_z)
        message(f"i{mark}4-", image(6, lane, 1), image(7, lane, 1), up_z)
        for slot in range(8):
            message(f"s{mark}{slot}", image(slot, lane), image(slot, lane), other_core)

    def copy(name):
        number, src, dst, to = messages[name]
        return pltpu.make_async_remote_copy(
            src_ref=src,
            dst_ref=dst,
            send_sem=send_sem.at[number],
            recv_sem=recv_sem.at[number],
            device_id=to,
            device_id_type=pl.DeviceIdType.MESH,
        )

    def start(*names):
        for name in names:
            copy(name).start()

    def got(*names):
        for name in names:
            if name[0] == "s":
                number, _, _, to = messages[name]
                slot, lane = int(name[2]), "oq".index(name[1])
                off = slot * SLOT + lane * 128 + (1 - core) * 64
                there = ib.at[:, pl.ds(pl.multiple_of(off, 32), 64), :]
                pltpu.make_async_remote_copy(
                    src_ref=there,
                    dst_ref=there,
                    send_sem=send_sem.at[number],
                    recv_sem=recv_sem.at[number],
                    device_id=to,
                    device_id_type=pl.DeviceIdType.MESH,
                ).wait_recv()
            else:
                copy(name).wait_recv()

    own_rows = pl.ds(pl.multiple_of(core * 64, 64), 64)
    loads = [
        (txt_l.at[0], tb.at[0, pl.ds(0, 2 * HALF), :]),
        (txt_r.at[0], tb.at[1, pl.ds(0, 2 * HALF), :]),
        (img_l, ib.at[0, own_rows, :]),
        (img_r, ib.at[1, own_rows, :]),
        (isc_l, isc.at[0, 0]),
        (isc_r, isc.at[0, 1]),
        (pair, ipr.at[0]),
        (tsc_l, tsc.at[0, 0]),
        (tsc_r, tsc.at[0, 1]),
    ]
    loads = [pltpu.make_async_copy(s, d, local_sem.at[i]) for i, (s, d) in enumerate(loads)]
    for load in loads:
        load.start()
    barrier = pltpu.get_barrier_semaphore()
    near = (up_x, dn_x, up_y, dn_y)
    for to in near + (up_z, dn_z, other_core, diag):
        pl.semaphore_signal(barrier, inc=1, device_id=to, device_id_type=pl.DeviceIdType.MESH)
    for load in loads:
        load.wait()
    pl.semaphore_wait(barrier, 8)
    start("t1p", "t2p", "ip", "tsc", "isc", "ipr")
    start("io1+", "io1-", "t1o-", "t1o+", "t2o-", "t2o+", "so0")

    def tell(r):
        for to in near:
            pl.semaphore_signal(ready.at[r], inc=1, device_id=to, device_id_type=pl.DeviceIdType.MESH)

    def told(r):
        pl.semaphore_wait(ready.at[r], 4)

    tell(0)

    def source(piece):
        if piece in (0, 1, 2, 3):
            dx, dy, lane, half = 0, 0, piece // 2, piece % 2
        elif piece < 12:
            lane, half = (piece - 4) // 4, ((piece - 4) // 2) % 2
            step = 1 - 2 * (piece % 2)
            dx, dy = (0, step) if half == 0 else (step, 0)
        else:
            lane, half = piece % 2, (piece - 12) // 2
            dx, dy = (0, 2) if half == 0 else (2, 0)
        px = x_pair if (lane == 1 and half == 0) else wrap(x + dx, 4)
        py = y_pair if (lane == 1 and half == 1) else wrap(y + dy, 4)
        same = (half == 0 and lane == 0) or (half == 1 and dx % 2 == 0)
        return px, py, half, same

    def spread(which):
        @pl.loop(0, 24)
        def _(i):
            k, q = lax.div(i, 12), lax.rem(i, 12)
            line = tsc[which, k, pl.ds(q, 1), :]
            bc[which, k, pl.ds(pl.multiple_of(q * 128, 128), 128), :] = jnp.transpose(
                jnp.broadcast_to(line, (128, 128))
            )

    def text_setup(which):
        for piece in range(16):
            px, py, half, same = source(piece)
            if same != (which == 0):
                continue
            off = (lax.div(px, 2) * 4 + py) * 192 + half * HALF
            block = (z * 2 + lax.rem(px, 2)) * 2 + core
            base[piece] = block * 1536 + off
            for k in range(2):
                tcol[k, pl.ds(piece * HALF, HALF), :] = bc[which, k, pl.ds(pl.multiple_of(off, 32), HALF), :]

    def image_setup(lane):
        odd = x_odd if lane == 0 else 1 - x_odd
        lanes = pl.ds(lane * 128, 128)
        for slot, dz in enumerate(SLOT_Z):
            at = pl.ds(wrap(z + dz, 8) * 2 + odd, 1)
            irow[slot, 0:1, lanes] = isc[lane, 0, at, :] * (4.0 * LOG2E)
            irow[slot, 1:2, lanes] = isc[lane, 1, at, :] * (6.0 * LOG2E)
            iprow[slot, 0:1, lanes] = ipr[lane, at, :]

    def tile(k):
        early, late = lax.div(k - 10, 5), lax.div(k - 20, 4)
        slot = jnp.where(k < 10, lax.div(k, 2), jnp.where(k < 20, k - 10 - 5 * early, 5 + late))
        chunk = jnp.where(k < 10, lax.rem(k, 2), jnp.where(k < 20, 2 + early, k - 20 - 4 * late))
        return slot, chunk

    def dots(k, dl, dr):
        slot, chunk = tile(k)
        rows = pl.ds(pl.multiple_of(chunk * CHUNK, CHUNK), CHUNK)
        cols = pl.ds(pl.multiple_of(slot * SLOT, SLOT), SLOT)
        for which, out in ((0, dl), (1, dr)):
            out[...] = lax.dot_general(
                tb[which, rows, :], ib[which, cols, :], (((1,), (1,)), ((), ())), preferred_element_type=F32
            )

    def scores(k, dl, dr):
        slot, chunk = tile(k)
        scale = irow[slot]
        a_learn = jnp.broadcast_to(scale[0:1], (8, SLOT))
        a_refer = jnp.broadcast_to(scale[1:2], (8, SLOT))
        wanted = jnp.broadcast_to(iprow[slot][0:1], (8, SLOT)) - lax.broadcasted_iota(jnp.int32, (8, SLOT), 0)
        total = rs[slot]
        for piece in range(4):
            here = wanted - base[chunk * 4 + piece]
            for g in range(HALF // 8):
                at = piece * HALF + g * 8
                rows = pl.ds(pl.multiple_of(chunk * CHUNK + at, 8), 8)
                b_learn, b_refer = tcol[0, rows, :], tcol[1, rows, :]
                d = score(
                    dl[at : at + 8, :],
                    dr[at : at + 8, :],
                    a_learn,
                    a_refer,
                    jnp.concatenate([b_learn, b_learn], axis=1),
                    jnp.concatenate([b_refer, b_refer], axis=1),
                    here == g * 8,
                    c_learn,
                    c_refer,
                )
                total = total + d
                cs[rows, :] = cs[rows, :] + (d[:, :128] + d[:, 128:])
        rs[slot] = total

    rs[...] = jnp.zeros_like(rs)
    cs[...] = jnp.zeros_like(cs)
    spread(0)
    text_setup(0)
    image_setup(0)

    def near_z():
        got("io1+", "io1-")
        start("io2+", "io2-", "so1", "so2")

    def diag_in():
        got("ip")
        start("iq1+", "iq1-", "sq0")

    def near_text():
        for name in ("t1", "t2"):
            got(name + "o-", name + "o+")
            start(name + "o2-", name + "o2+")

    def pair_text():
        got("t1p")
        start("t1q-", "t1q+")
        got("t2p")
        start("t2q-", "t2q+")

    def second_z():
        got("io2+", "io2-")
        start("io3+", "io3-", "so3", "so4")

    def near_q():
        got("iq1+", "iq1-")
        start("iq2+", "iq2-", "sq1", "sq2")

    def near_pair_text():
        for name in ("t1", "t2"):
            got(name + "q-", name + "q+")
            start(name + "q2-", name + "q2+")

    def third_z():
        got("io3+", "io3-")
        start("io4+", "io4-", "so5", "so6")

    def second_q():
        got("iq2+", "iq2-")
        start("iq3+", "iq3-", "sq3", "sq4")

    def far_text():
        for name in ("t1", "t2"):
            got(name + "o2-", name + "o2+", name + "q2-", name + "q2+")

    def third_q():
        got("iq3+", "iq3-")
        start("iq4+", "iq4-", "sq5", "sq6")

    def far_z():
        got("io4+", "io4-")
        start("so7")

    def far_q():
        got("iq4+", "iq4-")
        start("sq7")

    near_z()
    diag_in()
    got("tsc", "isc", "ipr")
    spread(1)
    text_setup(1)
    image_setup(1)
    near_text()
    pair_text()
    got("so0", "sq0")
    told(0)
    tell(1)

    def events(k):
        if k == 2:
            second_z()
            near_q()
            got("so1", "sq1")
        elif k == 4:
            got("so2", "sq2")
        elif k == 6:
            third_z()
            second_q()
            got("so3", "sq3")
            told(1)
            tell(2)
        elif k == 8:
            got("so4", "sq4")
        elif k == 10:
            near_pair_text()
        elif k == 12:
            third_q()
        elif k == 15:
            far_text()
        elif k == 16:
            far_z()
        elif k == 20:
            got("so5", "sq5")
        elif k == 24:
            got("so6", "sq6")
            told(2)
        elif k == 28:
            far_q()
            got("so7", "sq7")

    times = (2, 4, 6, 8, 10, 12, 15, 16, 20, 24, 28)

    def at_step(k, odd):
        for t in times:
            if t % 2 == odd:

                @pl.when(k == t)
                def _(t=t):
                    events(t)

    dots(0, dl0, dr0)

    @pl.loop(0, STEPS // 2 - 1)
    def _(i):
        at_step(2 * i + 1, 1)
        dots(2 * i + 1, dl1, dr1)
        scores(2 * i, dl0, dr0)
        at_step(2 * i + 2, 0)
        dots(2 * i + 2, dl0, dr0)
        scores(2 * i + 1, dl1, dr1)

    dots(STEPS - 1, dl1, dr1)
    scores(STEPS - 2, dl0, dr0)
    scores(STEPS - 1, dl1, dr1)

    def row_copy(slot, lane, which):
        number = (slot * 2 + lane) * 2 + which
        if lane == 0:
            to = device(dz=SLOT_Z[slot], at_core=core if which == 0 else 1 - core)
        else:
            to = device(dz=SLOT_Z[slot], at_x=x_diag, at_y=y_diag, at_core=core if which == 0 else 1 - core)
        return pltpu.make_async_remote_copy(
            src_ref=row_part.at[slot * 2 + lane],
            dst_ref=row_recv.at[number],
            send_sem=row_send.at[number],
            recv_sem=row_got.at[number],
            device_id=to,
            device_id_type=pl.DeviceIdType.MESH,
        )

    for slot in (7, 6, 5, 4, 3, 2, 1, 0):
        line = jnp.sum(rs[slot], axis=0, keepdims=True) * LN2
        row_part[slot * 2] = line[:, :128]
        row_part[slot * 2 + 1] = line[:, 128:]
        for lane in (1, 0):
            for which in (1, 0):
                if (slot, lane, which) != (0, 0, 0):
                    row_copy(slot, lane, which).start()

    mine = x * 4 + y
    for piece in range(16):
        px, py, half, same = source(piece)
        line = jnp.sum(jnp.transpose(cs[pl.ds(piece * HALF, HALF), :]), axis=0, keepdims=True) * LN2
        place = py if half == 0 else 4 + lax.div(px, 2) * 2 + lax.rem(py, 2)
        col_part[0 if same else 1, place, :, 0:HALF] = line

    def col_copy(dx, dy):
        number = dx * 4 + dy - 1
        return pltpu.make_async_remote_copy(
            src_ref=col_part.at[dx % 2],
            dst_ref=col_recv.at[mine],
            send_sem=col_send.at[number],
            recv_sem=col_got.at[number],
            device_id=device(dx=dx, dy=dy),
            device_id_type=pl.DeviceIdType.MESH,
        )

    plane = [(dx, dy) for dx in range(4) for dy in range(4) if (dx, dy) != (0, 0)]
    for dx, dy in sorted(plane, key=lambda d: -(min(d[0], 4 - d[0]) + min(d[1], 4 - d[1]))):
        col_copy(dx, dy).start()
    col_recv[mine] = col_part[0]
    row_recv[0] = row_part[0]

    for slot in range(8):
        for lane in range(2):
            for which in range(2):
                if (slot, lane, which) != (0, 0, 0):
                    row_copy(slot, lane, which).wait_recv()
    line = row_recv[0]
    for number in range(1, 32):
        line = line + row_recv[number]
    row_out[...] = jnp.where(core == 0, line[:, :64], line[:, 64:])
    for dx, dy in plane:
        col_copy(dx, dy).wait_recv()
    for x_hi in range(2):
        for yy in range(4):
            at = [(2 * x_hi + a) * 4 + b for a in range(2) for b in range(4)]
            col_out[pl.ds((x_hi * 4 + yy) * 2, 1), :] = functools.reduce(
                lambda s, t: s + t, [col_recv[n, yy] for n in at]
            )
        for y_hi in range(2):
            for y_low in range(2):
                at = [a * 4 + 2 * y_hi + b for a in range(4) for b in range(2)]
                col_out[pl.ds((x_hi * 4 + y_hi * 2 + y_low) * 2 + 1, 1), :] = functools.reduce(
                    lambda s, t: s + t, [col_recv[n, 4 + x_hi * 2 + y_low] for n in at]
                )

    for name in messages:
        copy(name).wait_send()
    for slot in range(8):
        for lane in range(2):
            for which in range(2):
                if (slot, lane, which) != (0, 0, 0):
                    row_copy(slot, lane, which).wait_send()
    for dx, dy in plane:
        col_copy(dx, dy).wait_send()


def shards(
    image_learn,
    image_refer,
    text_learn,
    text_refer,
    image_scale_learn,
    image_scale_refer,
    text_scale_learn,
    text_scale_refer,
    pair_index,
):
    offset = math.log(text_scale_learn.shape[0] * lax.axis_size("col"))
    vmem, dma = pltpu.VMEM, pltpu.SemaphoreType.DMA
    any_space = pl.BlockSpec(memory_space=pl.ANY)
    rows, cols = pl.pallas_call(
        functools.partial(kernel, (1.0 - offset) * LOG2E, (-1.0 - offset) * LOG2E),
        out_shape=[jax.ShapeDtypeStruct((1, 64), F32), jax.ShapeDtypeStruct((16, 128), F32)],
        in_specs=[any_space] * 9,
        out_specs=[pl.BlockSpec(memory_space=vmem)] * 2,
        scratch_shapes=[
            vmem((2, 4 * CHUNK, E), jnp.bfloat16),
            vmem((2, 8 * SLOT, E), jnp.bfloat16),
            vmem((2, 2, 16, 128), F32),
            vmem((2, 16, 128), jnp.int32),
            vmem((2, 2, 12, 128), F32),
            vmem((2, 2, 1536, 128), F32),
            vmem((2, 4 * CHUNK, 128), F32),
            vmem((8, 8, SLOT), F32),
            vmem((8, 8, SLOT), jnp.int32),
            pltpu.SMEM((16,), jnp.int32),
            vmem((8, 8, SLOT), F32),
            vmem((4 * CHUNK, 128), F32),
            vmem((CHUNK, SLOT), F32),
            vmem((CHUNK, SLOT), F32),
            vmem((CHUNK, SLOT), F32),
            vmem((CHUNK, SLOT), F32),
            vmem((16, 1, 128), F32),
            vmem((32, 1, 128), F32),
            vmem((2, 8, 1, 128), F32),
            vmem((16, 8, 1, 128), F32),
            dma((9,)),
            dma((54,)),
            dma((54,)),
            dma((32,)),
            dma((32,)),
            dma((15,)),
            dma((15,)),
            pltpu.SemaphoreType.REGULAR((3,)),
        ],
        compiler_params=pltpu.CompilerParams(
            collective_id=0, has_side_effects=True, vmem_limit_bytes=44 * 2**20
        ),
        cost_estimate=pl.CostEstimate(
            flops=4 * 2048 * 1536 * E, bytes_accessed=2**21, transcendentals=3 * 2048 * 1536
        ),
        name="gather_score",
    )(
        image_learn,
        image_refer,
        text_learn,
        text_refer,
        image_scale_learn.reshape(16, 128),
        image_scale_refer.reshape(16, 128),
        text_scale_learn.reshape(12, 128),
        text_scale_refer.reshape(12, 128),
        pair_index.reshape(16, 128),
    )
    return rows.reshape(64), cols[:, :HALF].reshape(1536)


def solution(mesh):
    in_specs = (
        P(("grp", "col"), None),
        P(("grp", "col"), None),
        P("col", "grp", None),
        P("col", "grp", None),
        P("grp"),
        P("grp"),
        P("col"),
        P("col"),
        P("grp"),
    )
    out_specs = (P(("grp", "col")), P("col"))
    return jax.shard_map(shards, mesh=mesh, in_specs=in_specs, out_specs=out_specs, check_vma=False)
```

time: 407 us -> 95.7 us (0.24)
  waiting for transfers between devices: 271 us -> 0 us
  Pallas kernels: 0 us -> 86.1 us
  blocking collectives: 74.5 us -> 0 us
  matrix products: 42.3 us -> 0 us
  between operations: 14.5 us -> 0.66 us
  local copies, waits for them, and re-layouts: 1.88 us -> 8.5 us
    all_gather x4 -> x0, waiting for transfers between devices: 268 us -> none  [the longest x1 73 us: shards(): lax.all_gather(text_learn, 'grp', axis=1, tiled=True)]
    pallas_call x0 -> x1, Pallas kernels: none -> 86.1 us  [shards(): pl.pallas_call(functools.partial(kernel, (1.0 - offset) * LOG2E, (-1.0 -...]
    unnamed x1 -> x0, blocking collectives: 53.6 us -> none
    dot_general x2 -> x0, matrix products: 42.3 us -> none  [inner(): lax.dot_general(left, right, (((1,), (1,)), ((), ())), preferred_element_...]
    psum x1 -> x0, blocking collectives: 20.9 us -> none  [shards(): col_part = lax.psum(col_local, 'grp')]
    unnamed x12 -> x19, local copies, waits for them, and re-layouts: 1.88 us -> 7.83 us
  transfers between devices with their start and end apart: 4 -> 0, of which waited for: 4 -> 0; matrix products, arithmetic and copies ran while one was open for 4% -> 0% of each run, Pallas kernels for 0% -> 0%
where the time goes in v1:
time: 95.7 us; the launch traced here: 95.2 us
  Pallas kernels  86.1 us (90%)
  local copies, waits for them, and re-layouts  8.5 us (9%)
    pallas_call x1, Pallas kernels, shards(): pl.pallas_call(functools.partial(kernel, (1.0 - offset) * LOG2E, (-1.0 -...  86.1 us
    unnamed x19, local copies, waits for them, and re-layouts  7.83 us

profile of v1, /device:TPU:1, one launch (start us, length us, event | category | flops | bytes accessed | tf_op | source)
XLA Modules:
  0.0 95.2 jit_solution(12772553057755359509)
XLA Ops:
  0.6 0.0 copy-start.4
  0.6 0.7 copy-done.4
  1.3 0.0 copy-start
  1.3 1.0 %copy-done = bf16[1,192,1152]{2,1,0:T(8,128)(2,1)S(1)} copy-done((bf16[1,192,1152]{2,1,0:T(8,128)(2,1)S(1)}, bf16[1,192,1152]{2,1,0:T(8,128)(2,1)}, u32[]{:S(2)}) %copy-start) | copy-done | bytes 442392
  2.3 0.0 copy-start.1
  2.3 1.0 %copy-done.1 = bf16[1,192,1152]{2,1,0:T(8,128)(2,1)S(1)} copy-done((bf16[1,192,1152]{2,1,0:T(8,128)(2,1)S(1)}, bf16[1,192,1152]{2,1,0:T(8,128)(2,1)}, u32[]{:S(2)}) %copy-start.1) | copy-done | bytes 442392
  3.4 0.0 copy-start.2
  3.4 0.9 copy-done.2
  4.3 0.0 copy-start.3
  4.3 0.9 copy-done.3
  5.2 0.0 copy-start.5
  5.2 0.7 copy-done.5
  5.9 0.0 copy-start.6
  5.9 0.7 copy-done.6
  6.6 0.0 copy-start.7
  6.6 0.7 copy-done.7
  7.3 0.0 copy-start.8
  7.3 0.7 copy-done.8
  8.0 86.1 %gather_score.1 = (f32[1,64]{1,0:T(1,128)S(1)}, f32[16,128]{1,0:T(8,128)S(1)}) custom-call(bf16[64,1152]{1,0:T(8,128)(2,1)S(1)} %copy-done.2, bf16[64,1152]{1,0:T(8,128)(2,1)S(1)} %copy-done.3, bf16[1,192,1152]{2,1,0:T(8,128)(2,1)S(1)} %copy-done, bf16[1,192,1152]{2,1,0:T(8,128)(2,1)S(1)} %copy-done.1, f32[16,128]{1,0:T(8,128)S(1)} %bitcast.8, ...), custom_call_target="tpu_custom_call" | custom-call | flops 14495514624 | bytes 2097152 | tf_op jit(solution)/shard_map/gather_score/pallas_call | solution.py:531
  94.1 0.7 reshape.31
  94.7 0.5 copy.12
Async XLA Ops:
  0.6 0.7 copy-start.4
  1.3 1.0 %copy-start = (bf16[1,192,1152]{2,1,0:T(8,128)(2,1)S(1)}, bf16[1,192,1152]{2,1,0:T(8,128)(2,1)}, u32[]{:S(2)}) copy-start(bf16[1,192,1152]{2,1,0:T(8,128)(2,1)} %txt_l.1) | copy-start | bytes 1327108
  2.3 1.0 %copy-start.1 = (bf16[1,192,1152]{2,1,0:T(8,128)(2,1)S(1)}, bf16[1,192,1152]{2,1,0:T(8,128)(2,1)}, u32[]{:S(2)}) copy-start(bf16[1,192,1152]{2,1,0:T(8,128)(2,1)} %txt_r.1) | copy-start | bytes 1327108
  3.4 0.9 copy-start.2
  4.3 0.9 copy-start.3
  5.2 0.7 copy-start.5
  5.9 0.7 copy-start.6
  6.6 0.7 copy-start.7
  7.3 0.7 copy-start.8

commit v2 on v1

v2 whole, which is shorter than its diff:
```python
import functools
import math

import jax
import jax.numpy as jnp
from jax import lax
from jax.experimental import pallas as pl
from jax.experimental.pallas import tpu as pltpu
from jax.sharding import PartitionSpec as P

F32 = jnp.float32
LOG2E = 1.0 / math.log(2.0)
LN2 = math.log(2.0)
SERIES = tuple(2.0 * LOG2E * c for c in (0.99999984, 0.33337989, 0.1979503, 0.17111227))

E = 1152
HALF = 96
CHUNK = 4 * HALF
BLOCK = 256
PIECE_Z = (0, 0, 1, -1, 1, -1, 2, -2, 2, -2, 3, -3, 3, -3, 4, 4)
PIECE_LANE = (0, 1, 0, 0, 1, 1, 0, 0, 1, 1, 0, 0, 1, 1, 0, 1)
STEPS = 32


def wrap(value, size):
    return lax.rem(value + size, size)


def score(dot_learn, dot_refer, a_learn, a_refer, b_learn, b_refer, paired, c_learn, c_refer):
    u = dot_learn * a_learn * b_learn + c_learn
    w = dot_refer * a_refer * b_refer + c_refer
    p = jnp.exp2(-jnp.abs(u))
    q = jnp.exp2(-jnp.abs(w))
    z = (p - q) * pl.reciprocal((p + q) + 2.0, approx=True)
    s = z * z
    poly = s * SERIES[3] + SERIES[2]
    poly = poly * s + SERIES[1]
    poly = poly * s + SERIES[0]
    d = (jnp.maximum(u, 0.0) - jnp.maximum(w, 0.0)) + z * poly
    return d - jnp.where(paired, u - w, 0.0)


def kernel(
    c_learn,
    c_refer,
    img_l,
    img_r,
    txt_l,
    txt_r,
    isc_l,
    isc_r,
    tsc_l,
    tsc_r,
    pair,
    row_out,
    col_out,
    tb,
    ib,
    isc,
    ipr,
    tsc,
    bc,
    tcol,
    irow,
    iprow,
    base,
    rs,
    cs,
    dl0,
    dr0,
    dl1,
    dr1,
    row_part,
    row_recv,
    col_part,
    col_recv,
    local_sem,
    send_sem,
    recv_sem,
    row_sem,
    col_sem,
    ready,
):
    grp, col = lax.axis_index("grp"), lax.axis_index("col")
    x = lax.div(grp, 4) * 2 + lax.rem(lax.div(col, 2), 2)
    y = lax.rem(grp, 4)
    z = lax.div(col, 4)
    core = lax.rem(col, 2)
    x_odd, y_odd = lax.rem(x, 2), lax.rem(y, 2)
    x_pair, y_pair = x + 1 - 2 * x_odd, y + 1 - 2 * y_odd
    x_diag, y_diag = wrap(x - 1 + 2 * x_odd, 4), wrap(y - 1 + 2 * y_odd, 4)

    def device(dx=0, dy=0, dz=0, at_x=None, at_y=None, at_core=None):
        px = wrap(x + dx, 4) if at_x is None else at_x
        py = wrap(y + dy, 4) if at_y is None else at_y
        pz = wrap(z + dz, 8)
        pc = core if at_core is None else at_core
        return lax.div(px, 2) * 4 + py, (pz * 2 + lax.rem(px, 2)) * 2 + pc

    other_core = device(at_core=1 - core)
    diag = device(at_x=x_diag, at_y=y_diag)
    pair_x, next_x = device(at_x=x_pair), device(at_x=x_diag)
    pair_y, next_y = device(at_y=y_pair), device(at_y=y_diag)
    up_z, dn_z = device(dz=1), device(dz=-1)

    messages = {}

    def message(name, src, dst, to):
        messages[name] = (len(messages), src, dst, to)

    def text(piece, part=None):
        off, rows = (piece * HALF, HALF) if part is None else (piece * HALF + part * (HALF // 2), HALF // 2)
        return tb.at[:, pl.ds(off, rows), :]

    def image(piece, part=None):
        rows = 64 if part is None else 32
        off = piece * 128 + core * 64 + (0 if part is None else part * 32)
        return ib.at[:, pl.ds(pl.multiple_of(off, 32), rows), :]

    message("tsc", tsc.at[0], tsc.at[1], pair_x)
    message("isc", isc.at[0], isc.at[1], diag)
    message("ipr", ipr.at[0], ipr.at[1], diag)
    message("t1p", text(0), text(2), pair_x)
    message("t2p", text(1), text(3), pair_y)
    message("ip", image(0), image(1), diag)
    for name, first, to_p, to_n in (("t1", 0, pair_y, next_y), ("t2", 1, pair_x, next_x)):
        o, far = 4 + 2 * first, 12 + first
        message(name + "oP", text(first), text(o), to_p)
        message(name + "oN", text(first), text(o + 1), to_n)
        message(name + "qP", text(2 + first), text(o + 4), to_p)
        message(name + "qN", text(2 + first), text(o + 5), to_n)
        message(name + "o2A", text(o, 0), text(far, 0), to_n)
        message(name + "o2B", text(o + 1, 1), text(far, 1), to_p)
        message(name + "q2A", text(o + 4, 0), text(far + 2, 0), to_n)
        message(name + "q2B", text(o + 5, 1), text(far + 2, 1), to_p)
    for lane, mark in ((0, "o"), (1, "q")):
        place = {dz: p for p, dz in enumerate(PIECE_Z) if PIECE_LANE[p] == lane}
        for k in (1, 2, 3):
            message(f"i{mark}{k}+", image(place[k - 1]), image(place[k]), dn_z)
            message(f"i{mark}{k}-", image(place[1 - k]), image(place[-k]), up_z)
        message(f"i{mark}4+", image(place[3], 0), image(place[4], 0), dn_z)
        message(f"i{mark}4-", image(place[-3], 1), image(place[4], 1), up_z)
    for piece in range(16):
        message(f"s{piece}", image(piece), image(piece), other_core)

    def sender(name):
        return {"tsc": 2, "isc": 3, "ipr": 4}.get(name, 0 if name[0] == "t" else 1)

    def copy(name):
        number, src, dst, to = messages[name]
        return pltpu.make_async_remote_copy(
            src_ref=src,
            dst_ref=dst,
            send_sem=send_sem.at[sender(name)],
            recv_sem=recv_sem.at[number],
            device_id=to,
            device_id_type=pl.DeviceIdType.MESH,
        )

    def start(*names):
        for name in names:
            copy(name).start()

    def got(*names):
        for name in names:
            if name[0] == "s":
                number, _, _, to = messages[name]
                off = int(name[1:]) * 128 + (1 - core) * 64
                there = ib.at[:, pl.ds(pl.multiple_of(off, 32), 64), :]
                pltpu.make_async_remote_copy(
                    src_ref=there,
                    dst_ref=there,
                    send_sem=send_sem.at[sender(name)],
                    recv_sem=recv_sem.at[number],
                    device_id=to,
                    device_id_type=pl.DeviceIdType.MESH,
                ).wait_recv()
            else:
                copy(name).wait_recv()

    own_rows = pl.ds(pl.multiple_of(core * 64, 64), 64)
    loads = [
        (0, txt_l.at[0], tb.at[0, pl.ds(0, 2 * HALF), :]),
        (0, txt_r.at[0], tb.at[1, pl.ds(0, 2 * HALF), :]),
        (1, img_l, ib.at[0, own_rows, :]),
        (1, img_r, ib.at[1, own_rows, :]),
        (2, isc_l, isc.at[0, 0]),
        (2, isc_r, isc.at[0, 1]),
        (3, tsc_l, tsc.at[0, 0]),
        (3, tsc_r, tsc.at[0, 1]),
        (4, pair, ipr.at[0]),
    ]
    for number, src, dst in loads:
        pltpu.make_async_copy(src, dst, local_sem.at[number]).start()

    def all_of(ref, sem):
        pltpu.make_async_copy(ref, ref, sem).wait()

    barrier = pltpu.get_barrier_semaphore()
    near = (pair_x, next_x, pair_y, next_y)
    for to in near + (up_z, dn_z, other_core, diag):
        pl.semaphore_signal(barrier, inc=1, device_id=to, device_id_type=pl.DeviceIdType.MESH)
    for number, ref in enumerate((tb.at[:, pl.ds(0, 2 * HALF), :], ib.at[:, own_rows, :], isc.at[0], tsc.at[0], ipr.at[0])):
        all_of(ref, local_sem.at[number])
    pl.semaphore_wait(barrier, 8)
    start("tsc", "isc", "ipr", "t1p", "t2p", "ip", "io1+", "io1-", "t1oP", "t2oP", "s0")

    def tell(r):
        for to in near:
            pl.semaphore_signal(ready.at[r], inc=1, device_id=to, device_id_type=pl.DeviceIdType.MESH)

    def told(r):
        pl.semaphore_wait(ready.at[r], 4)

    tell(0)

    def source(piece):
        if piece < 4:
            lane, half, side = piece // 2, piece % 2, 0
        elif piece < 12:
            lane, half, side = (piece - 4) // 4, ((piece - 4) // 2) % 2, 1 + piece % 2
        else:
            lane, half, side = (piece - 12) // 2, piece % 2, 3
        along_x, along_y = (x, x_pair, x_diag, wrap(x + 2, 4)), (y, y_pair, y_diag, wrap(y + 2, 4))
        px = along_x[side] if half == 1 else along_x[lane]
        py = along_y[side] if half == 0 else along_y[lane]
        same = lane == 0 if half == 0 else side in (0, 3)
        return px, py, half, same

    def spread(which):
        @pl.loop(0, 24)
        def _(i):
            k, q = lax.div(i, 12), lax.rem(i, 12)
            line = tsc[which, k, pl.ds(q, 1), :]
            bc[which, k, pl.ds(pl.multiple_of(q * 128, 128), 128), :] = jnp.transpose(
                jnp.broadcast_to(line, (128, 128))
            )

    def text_setup(which):
        for piece in range(16):
            px, py, half, same = source(piece)
            if same != (which == 0):
                continue
            off = (lax.div(px, 2) * 4 + py) * 192 + half * HALF
            block = (z * 2 + lax.rem(px, 2)) * 2 + core
            base[piece] = block * 1536 + off
            for k in range(2):
                tcol[k, pl.ds(piece * HALF, HALF), :] = bc[which, k, pl.ds(pl.multiple_of(off, 32), HALF), :]

    def image_setup(lane):
        odd = x_odd if lane == 0 else 1 - x_odd
        for piece in range(16):
            if PIECE_LANE[piece] != lane:
                continue
            block, lanes = piece // 2, pl.ds((piece % 2) * 128, 128)
            at = pl.ds(wrap(z + PIECE_Z[piece], 8) * 2 + odd, 1)
            irow[block, 0:1, lanes] = isc[lane, 0, at, :] * (4.0 * LOG2E)
            irow[block, 1:2, lanes] = isc[lane, 1, at, :] * (6.0 * LOG2E)
            iprow[block, 0:1, lanes] = ipr[lane, at, :]

    def tile(k):
        block = jnp.where(
            k < 18,
            jnp.where(
                k < 8,
                jnp.where(k < 6, lax.rem(k, 3), 3),
                jnp.where(k < 12, k - 8, lax.div(k, 3)),
            ),
            jnp.where(k < 26, jnp.where(k < 22, k - 18, 6), jnp.where(k < 28, k - 22, 7)),
        )
        chunk = jnp.where(
            k < 18,
            jnp.where(k < 8, jnp.where(k < 6, lax.div(k, 3), k - 6), jnp.where(k < 12, 2, lax.rem(k, 3))),
            jnp.where(k < 26, jnp.where(k < 22, 3, k - 22), jnp.where(k < 28, 3, k - 28)),
        )
        return block, chunk

    def dots(k, dl, dr):
        block, chunk = tile(k)
        rows = pl.ds(pl.multiple_of(chunk * CHUNK, CHUNK), CHUNK)
        cols = pl.ds(pl.multiple_of(block * BLOCK, BLOCK), BLOCK)
        for which, out in ((0, dl), (1, dr)):
            out[...] = lax.dot_general(
                tb[which, rows, :], ib[which, cols, :], (((1,), (1,)), ((), ())), preferred_element_type=F32
            )

    def scores(k, dl, dr):
        block, chunk = tile(k)
        scale = irow[block]
        a_learn = jnp.broadcast_to(scale[0:1], (8, BLOCK))
        a_refer = jnp.broadcast_to(scale[1:2], (8, BLOCK))
        wanted = jnp.broadcast_to(iprow[block][0:1], (8, BLOCK)) - lax.broadcasted_iota(jnp.int32, (8, BLOCK), 0)
        total = rs[block]
        for piece in range(4):
            here = wanted - base[chunk * 4 + piece]
            for g in range(HALF // 8):
                at = piece * HALF + g * 8
                rows = pl.ds(pl.multiple_of(chunk * CHUNK + at, 8), 8)
                b_learn, b_refer = tcol[0, rows, :], tcol[1, rows, :]
                d = score(
                    dl[at : at + 8, :],
                    dr[at : at + 8, :],
                    a_learn,
                    a_refer,
                    jnp.concatenate([b_learn, b_learn], axis=1),
                    jnp.concatenate([b_refer, b_refer], axis=1),
                    here == g * 8,
                    c_learn,
                    c_refer,
                )
                total = total + d
                cs[rows, :] = cs[rows, :] + (d[:, :128] + d[:, 128:])
        rs[block] = total

    rs[...] = jnp.zeros_like(rs)
    cs[...] = jnp.zeros_like(cs)
    spread(0)
    text_setup(0)
    image_setup(0)

    def row_copy(piece, which):
        number = piece * 2 + which
        at_core = core if which == 0 else 1 - core
        if PIECE_LANE[piece] == 0:
            to = device(dz=PIECE_Z[piece], at_core=at_core)
        else:
            to = device(dz=PIECE_Z[piece], at_x=x_diag, at_y=y_diag, at_core=at_core)
        return pltpu.make_async_remote_copy(
            src_ref=row_part.at[piece],
            dst_ref=row_recv.at[number],
            send_sem=row_sem.at[0],
            recv_sem=row_sem.at[1],
            device_id=to,
            device_id_type=pl.DeviceIdType.MESH,
        )

    row_messages = [(piece, which) for piece in range(16) for which in range(2) if (piece, which) != (0, 0)]

    def send_rows(blocks):
        for block in blocks:
            line = jnp.sum(rs[block], axis=0, keepdims=True) * LN2
            row_part[block * 2] = line[:, :128]
            row_part[block * 2 + 1] = line[:, 128:]
        for piece, which in reversed(row_messages):
            if piece // 2 in blocks:
                row_copy(piece, which).start()

    got("tsc", "isc", "ipr")
    spread(1)
    text_setup(1)
    image_setup(1)
    got("io1+", "io1-")
    start("s2", "s3")
    got("ip")
    start("iq1+", "iq1-", "io2+", "io2-", "s1", "t1oN", "t2oN")
    told(0)
    tell(1)
    got("t1p", "t2p")
    start("t1qP", "t2qP", "t1qN", "t2qN")
    got("s0", "s1", "s2", "s3")

    def events(i):
        if i == 1:
            got("iq1+", "iq1-")
            start("iq2+", "iq2-", "s4", "s5")
            got("t1oN", "t2oN")
            start("t1o2B", "t2o2B")
            got("t1oP", "t2oP")
            start("t1o2A", "t2o2A")
            got("s4", "s5")
        elif i == 2:
            got("io2+", "io2-")
            start("io3+", "io3-", "s6", "s7")
        elif i == 3:
            got("s6", "s7")
            told(1)
            tell(2)
        elif i == 4:
            got("t1qN", "t2qN")
            start("t1q2B", "t2q2B")
            got("iq2+", "iq2-")
            start("iq3+", "iq3-", "s8", "s9")
            got("t1qP", "t2qP")
            start("t1q2A", "t2q2A")
        elif i == 6:
            got("s8", "s9")
        elif i == 7:
            got("io3+", "io3-")
            start("io4+", "io4-", "s10", "s11")
            got("s10", "s11")
        elif i == 9:
            got("t1o2A", "t1o2B", "t2o2A", "t2o2B", "t1q2A", "t1q2B", "t2q2A", "t2q2B")
        elif i == 10:
            got("iq3+", "iq3-")
            start("iq4+", "iq4-", "s12", "s13")
        elif i == 11:
            got("s12", "s13")
        elif i == 12:
            got("io4+", "io4-")
            start("s14")
        elif i == 13:
            told(2)
        elif i == 14:
            send_rows((0, 1, 2, 3, 4, 6))
            got("iq4+", "iq4-")
            start("s15")
            got("s14", "s15")

    dots(0, dl0, dr0)
    dots(1, dl1, dr1)
    scores(0, dl0, dr0)

    @pl.loop(1, STEPS // 2)
    def _(i):
        for low, high in ((1, 4), (4, 10), (10, 15)):

            @pl.when((i >= low) & (i < high))
            def _(low=low, high=high):
                for at in range(low, high):
                    if at not in (5, 8):

                        @pl.when(i == at)
                        def _(at=at):
                            events(at)

        dots(2 * i, dl0, dr0)
        scores(2 * i - 1, dl1, dr1)
        dots(2 * i + 1, dl1, dr1)
        scores(2 * i, dl0, dr0)

    scores(STEPS - 1, dl1, dr1)

    send_rows((5, 7))

    mine = x * 4 + y
    for piece in range(16):
        px, py, half, same = source(piece)
        line = jnp.sum(jnp.transpose(cs[pl.ds(piece * HALF, HALF), :]), axis=0, keepdims=True) * LN2
        place = py if half == 0 else 4 + lax.div(px, 2) * 2 + lax.rem(py, 2)
        col_part[0 if same else 1, place, :, 0:HALF] = line

    def col_copy(dx, dy):
        return pltpu.make_async_remote_copy(
            src_ref=col_part.at[dx % 2],
            dst_ref=col_recv.at[mine],
            send_sem=col_sem.at[0],
            recv_sem=col_sem.at[1],
            device_id=device(dx=dx, dy=dy),
            device_id_type=pl.DeviceIdType.MESH,
        )

    plane = [(dx, dy) for dx in range(4) for dy in range(4) if (dx, dy) != (0, 0)]
    for dx, dy in sorted(plane, key=lambda d: -(min(d[0], 4 - d[0]) + min(d[1], 4 - d[1]))):
        col_copy(dx, dy).start()
    col_recv[mine] = col_part[0]
    row_recv[0] = row_part[0]

    all_of(row_recv.at[pl.ds(0, 31)], row_sem.at[1])
    line = row_recv[0]
    for number in range(1, 32):
        line = line + row_recv[number]
    row_out[...] = jnp.where(core == 0, line[:, :64], line[:, 64:])
    all_of(col_recv.at[pl.ds(0, 15)], col_sem.at[1])
    for x_hi in range(2):
        for yy in range(4):
            at = [(2 * x_hi + a) * 4 + b for a in range(2) for b in range(4)]
            col_out[pl.ds((x_hi * 4 + yy) * 2, 1), :] = functools.reduce(
                lambda s, t: s + t, [col_recv[n, yy] for n in at]
            )
        for y_hi in range(2):
            for y_low in range(2):
                at = [a * 4 + 2 * y_hi + b for a in range(4) for b in range(2)]
                col_out[pl.ds((x_hi * 4 + y_hi * 2 + y_low) * 2 + 1, 1), :] = functools.reduce(
                    lambda s, t: s + t, [col_recv[n, 4 + x_hi * 2 + y_low] for n in at]
                )

    all_of(tb.at[:, pl.ds(0, 14 * HALF), :], send_sem.at[0])
    all_of(ib.at[:, pl.ds(0, 31 * 64), :], send_sem.at[1])
    all_of(tsc.at[0], send_sem.at[2])
    all_of(isc.at[0], send_sem.at[3])
    all_of(ipr.at[0], send_sem.at[4])
    all_of(row_recv.at[pl.ds(0, 31)], row_sem.at[0])
    all_of(col_recv.at[pl.ds(0, 15)], col_sem.at[0])


def shards(
    image_learn,
    image_refer,
    text_learn,
    text_refer,
    image_scale_learn,
    image_scale_refer,
    text_scale_learn,
    text_scale_refer,
    pair_index,
):
    offset = math.log(text_scale_learn.shape[0] * lax.axis_size("col"))
    vmem, dma = pltpu.VMEM, pltpu.SemaphoreType.DMA
    in_hbm = pl.BlockSpec(memory_space=pltpu.HBM)
    rows, cols = pl.pallas_call(
        functools.partial(kernel, (1.0 - offset) * LOG2E, (-1.0 - offset) * LOG2E),
        out_shape=[jax.ShapeDtypeStruct((1, 64), F32), jax.ShapeDtypeStruct((16, 128), F32)],
        in_specs=[in_hbm] * 9,
        out_specs=[pl.BlockSpec(memory_space=vmem)] * 2,
        scratch_shapes=[
            vmem((2, 4 * CHUNK, E), jnp.bfloat16),
            vmem((2, 8 * BLOCK, E), jnp.bfloat16),
            vmem((2, 2, 16, 128), F32),
            vmem((2, 16, 128), jnp.int32),
            vmem((2, 2, 12, 128), F32),
            vmem((2, 2, 1536, 128), F32),
            vmem((2, 4 * CHUNK, 128), F32),
            vmem((8, 8, BLOCK), F32),
            vmem((8, 8, BLOCK), jnp.int32),
            pltpu.SMEM((16,), jnp.int32),
            vmem((8, 8, BLOCK), F32),
            vmem((4 * CHUNK, 128), F32),
            vmem((CHUNK, BLOCK), F32),
            vmem((CHUNK, BLOCK), F32),
            vmem((CHUNK, BLOCK), F32),
            vmem((CHUNK, BLOCK), F32),
            vmem((16, 1, 128), F32),
            vmem((32, 1, 128), F32),
            vmem((2, 8, 1, 128), F32),
            vmem((16, 8, 1, 128), F32),
            dma((5,)),
            dma((5,)),
            dma((54,)),
            dma((2,)),
            dma((2,)),
            pltpu.SemaphoreType.REGULAR((3,)),
        ],
        compiler_params=pltpu.CompilerParams(
            collective_id=0, has_side_effects=True, vmem_limit_bytes=60 * 2**20
        ),
        cost_estimate=pl.CostEstimate(
            flops=4 * 2048 * 1536 * E, bytes_accessed=2**21, transcendentals=3 * 2048 * 1536
        ),
        name="gather_score",
    )(
        image_learn,
        image_refer,
        text_learn,
        text_refer,
        image_scale_learn.reshape(16, 128),
        image_scale_refer.reshape(16, 128),
        text_scale_learn.reshape(12, 128),
        text_scale_refer.reshape(12, 128),
        pair_index.reshape(16, 128),
    )
    return rows.reshape(64), cols[:, :HALF].reshape(1536)


def solution(mesh):
    in_specs = (
        P(("grp", "col"), None),
        P(("grp", "col"), None),
        P("col", "grp", None),
        P("col", "grp", None),
        P("grp"),
        P("grp"),
        P("col"),
        P("col"),
        P("grp"),
    )
    out_specs = (P(("grp", "col")), P("col"))
    return jax.shard_map(shards, mesh=mesh, in_specs=in_specs, out_specs=out_specs, check_vma=False)
```

time: 95.7 us -> 76.6 us (0.80)
  Pallas kernels: 86.1 us -> 73.9 us
  local copies, waits for them, and re-layouts: 8.5 us -> 1.88 us
    pallas_call x1, Pallas kernels: 86.1 us -> 73.9 us  [shards(): pl.pallas_call(functools.partial(kernel, (1.0 - offset) * LOG2E, (-1.0 -...]
    unnamed x19 -> x3, local copies, waits for them, and re-layouts: 7.83 us -> 0.52 us
where the time goes in v2:
time: 76.6 us; the launch traced here: 76.4 us
  Pallas kernels  73.9 us (96%)
  local copies, waits for them, and re-layouts  1.88 us (2%)
    pallas_call x1, Pallas kernels, shards(): pl.pallas_call(functools.partial(kernel, (1.0 - offset) * LOG2E, (-1.0 -...  73.9 us

profile of v2, /device:TPU:1, one launch (start us, length us, event | category | flops | bytes accessed | tf_op | source)
XLA Modules:
  0.0 76.4 jit_solution(16995731048261638795)
XLA Ops:
  0.6 73.9 %gather_score.1 = (f32[1,64]{1,0:T(1,128)}, f32[16,128]{1,0:T(8,128)}) custom-call(bf16[64,1152]{1,0:T(8,128)(2,1)} %img_l.1, bf16[64,1152]{1,0:T(8,128)(2,1)} %img_r.1, bf16[1,192,1152]{2,1,0:T(8,128)(2,1)} %txt_l.1, bf16[1,192,1152]{2,1,0:T(8,128)(2,1)} %txt_r.1, f32[16,128]{1,0:T(8,128)} %bitcast.8, f32[16,128]{1,0:T(8,128)} %bitcast.9, ...), custom_call_target="tpu_custom_call" | custom-call | flops 14495514624 | bytes 2097152 | tf_op jit(solution)/shard_map/gather_score/pallas_call | solution.py:500
  74.6 0.0 copy-start
  74.6 1.4 %reshape.31 = f32[1536]{0:T(1024)} reshape(f32[16,96]{1,0:T(8,128)} %bitcast.7) | data formatting | bytes 12288 | tf_op jit(solution)/shard_map/reshape | solution.py:551
  75.9 0.0 copy-done
  75.9 0.5 copy.12
Async XLA Ops:
  74.6 1.4 %copy-start = (f32[1,64]{1,0:T(1,128)S(1)}, f32[1,64]{1,0:T(1,128)}, u32[]{:S(2)}) copy-start(f32[1,64]{1,0:T(1,128)} %get-tuple-element.4) | copy-start | bytes 772

commit v3 on v2

--- a/solution.py
+++ b/solution.py
@@ -16,6 +16,7 @@
 E = 1152
 HALF = 96
 CHUNK = 4 * HALF
+SPLIT = {1: 1024, 2: 1024, 3: 1024, 4: 1024}
 BLOCK = 256
 PIECE_Z = (0, 0, 1, -1, 1, -1, 2, -2, 2, -2, 3, -3, 3, -3, 4, 4)
 PIECE_LANE = (0, 1, 0, 0, 1, 1, 0, 0, 1, 1, 0, 0, 1, 1, 0, 1)
@@ -103,82 +104,107 @@
     pair_y, next_y = device(at_y=y_pair), device(at_y=y_diag)
     up_z, dn_z = device(dz=1), device(dz=-1)
 
-    messages = {}
-
-    def message(name, src, dst, to):
-        messages[name] = (len(messages), src, dst, to)
-
-    def text(piece, part=None):
-        off, rows = (piece * HALF, HALF) if part is None else (piece * HALF + part * (HALF // 2), HALF // 2)
-        return tb.at[:, pl.ds(off, rows), :]
-
-    def image(piece, part=None):
+    groups, messages = {}, {}
+
+    def group(name, ref):
+        groups[name] = (len(groups), ref)
+
+    def message(name, group_name, copies, to):
+        messages[name] = (group_name, copies, to)
+
+    def text(piece, start=0, rows=HALF):
+        return tb.at[:, pl.ds(piece * HALF + start, rows), :]
+
+    def image(piece, part=None, first=0, size=E):
         rows = 64 if part is None else 32
         off = piece * 128 + core * 64 + (0 if part is None else part * 32)
-        return ib.at[:, pl.ds(pl.multiple_of(off, 32), rows), :]
-
-    message("tsc", tsc.at[0], tsc.at[1], pair_x)
-    message("isc", isc.at[0], isc.at[1], diag)
-    message("ipr", ipr.at[0], ipr.at[1], diag)
-    message("t1p", text(0), text(2), pair_x)
-    message("t2p", text(1), text(3), pair_y)
-    message("ip", image(0), image(1), diag)
+        return ib.at[:, pl.ds(pl.multiple_of(off, 32), rows), pl.ds(first, size)]
+
+    group("scales", bc.at[0, 0, pl.ds(0, 72), :])
+    message("tsc", "scales", [(tsc_l, tsc.at[1, 0]), (tsc_r, tsc.at[1, 1])], pair_x)
+    message("isc", "scales", [(isc_l, isc.at[1, 0]), (isc_r, isc.at[1, 1]), (pair, ipr.at[1])], diag)
+    group("tp", tb.at[:, pl.ds(0, 192), :])
+    first, second = pl.ds(0, HALF), pl.ds(HALF, HALF)
+    message("t1p", "tp", [(t.at[0, first, :], text(2).at[i]) for i, t in enumerate((txt_l, txt_r))], pair_x)
+    message("t2p", "tp", [(t.at[0, second, :], text(3).at[i]) for i, t in enumerate((txt_l, txt_r))], pair_y)
+    group("ip", ib.at[:, pl.ds(0, 64), :])
+    message("ip", "ip", [(r, image(1).at[i]) for i, r in enumerate((img_l, img_r))], diag)
+    for name in ("oP", "oN", "qP", "qN"):
+        group("t" + name, tb.at[:, pl.ds(0, 192), :])
+    group("t2", tb.at[:, pl.ds(0, 384), :])
     for name, first, to_p, to_n in (("t1", 0, pair_y, next_y), ("t2", 1, pair_x, next_x)):
         o, far = 4 + 2 * first, 12 + first
-        message(name + "oP", text(first), text(o), to_p)
-        message(name + "oN", text(first), text(o + 1), to_n)
-        message(name + "qP", text(2 + first), text(o + 4), to_p)
-        message(name + "qN", text(2 + first), text(o + 5), to_n)
-        message(name + "o2A", text(o, 0), text(far, 0), to_n)
-        message(name + "o2B", text(o + 1, 1), text(far, 1), to_p)
-        message(name + "q2A", text(o + 4, 0), text(far + 2, 0), to_n)
-        message(name + "q2B", text(o + 5, 1), text(far + 2, 1), to_p)
+        message(name + "oP", "toP", [(text(first), text(o))], to_p)
+        for part, start_row, rows in (("a", 0, 32), ("b", 32, 64)):
+            message(name + "oN" + part, "toN", [(text(first, start_row, rows), text(o + 1, start_row, rows))], to_n)
+        message(name + "qP", "tqP", [(text(2 + first), text(o + 4))], to_p)
+        message(name + "qN", "tqN", [(text(2 + first), text(o + 5))], to_n)
+        message(name + "o2A", "t2", [(text(o, 0, 48), text(far, 0, 48))], to_n)
+        message(name + "o2B", "t2", [(text(o + 1, 48, 48), text(far, 48, 48))], to_p)
+        message(name + "q2A", "t2", [(text(o + 4, 0, 48), text(far + 2, 0, 48))], to_n)
+        message(name + "q2B", "t2", [(text(o + 5, 48, 48), text(far + 2, 48, 48))], to_p)
     for lane, mark in ((0, "o"), (1, "q")):
         place = {dz: p for p, dz in enumerate(PIECE_Z) if PIECE_LANE[p] == lane}
-        for k in (1, 2, 3):
-            message(f"i{mark}{k}+", image(place[k - 1]), image(place[k]), dn_z)
-            message(f"i{mark}{k}-", image(place[1 - k]), image(place[-k]), up_z)
-        message(f"i{mark}4+", image(place[3], 0), image(place[4], 0), dn_z)
-        message(f"i{mark}4-", image(place[-3], 1), image(place[4], 1), up_z)
+        for k in (1, 2, 3, 4):
+            size = E if lane == 0 else SPLIT[k]
+            ring = f"i{mark}{k}"
+            if ring != "io1":
+                group(ring, ib.at[:, pl.ds(0, 128 if k < 4 else 64), pl.ds(0, size)])
+            if ring in ("io1", "io2"):
+                for i, (part, own) in enumerate((("l", img_l), ("r", img_r))):
+                    if ring == "io1":
+                        group(ring + part, ib.at[0, pl.ds(0, 128), :])
+                    for sign, to, at in (("+", dn_z, 1), ("-", up_z, -1)):
+                        src = own if ring == "io1" else image(place[at]).at[i]
+                        group_name = ring + part if ring == "io1" else ring
+                        message(ring + part + sign, group_name, [(src, image(place[k * at]).at[i])], to)
+            elif k < 4:
+                message(ring + "+", ring, [(image(place[k - 1], size=size), image(place[k], size=size))], dn_z)
+                message(ring + "-", ring, [(image(place[1 - k], size=size), image(place[-k], size=size))], up_z)
+            else:
+                message(ring + "+", ring, [(image(place[3], 0, size=size), image(place[4], 0, size=size))], dn_z)
+                message(ring + "-", ring, [(image(place[-3], 1, size=size), image(place[4], 1, size=size))], up_z)
+            if lane == 0 and SPLIT[k] < E:
+                rest = dict(first=SPLIT[k], size=E - SPLIT[k])
+                group(f"x{k}", ib.at[:, pl.ds(0, 128 if k < 4 else 64), pl.ds(0, E - SPLIT[k])])
+                for at in (k, -k) if k < 4 else (k,):
+                    there = [p for p in range(16) if PIECE_Z[p] == at and PIECE_LANE[p] == 1][0]
+                    message(f"x{k}{at}", f"x{k}", [(image(place[at], **rest), image(there, **rest))], diag)
+    for block in range(8):
+        if block != 1:
+            group(f"s{block}", ib.at[:, pl.ds(0, 128 if block else 256), :])
     for piece in range(16):
-        message(f"s{piece}", image(piece), image(piece), other_core)
+        message(f"s{piece}", f"s{piece // 2 if piece > 3 else 0}", [(image(piece), image(piece))], other_core)
 
     def sender(name):
-        return {"tsc": 2, "isc": 3, "ipr": 4}.get(name, 0 if name[0] == "t" else 1)
-
-    def copy(name):
-        number, src, dst, to = messages[name]
-        return pltpu.make_async_remote_copy(
-            src_ref=src,
-            dst_ref=dst,
-            send_sem=send_sem.at[sender(name)],
-            recv_sem=recv_sem.at[number],
-            device_id=to,
-            device_id_type=pl.DeviceIdType.MESH,
-        )
+        return 2 if name in ("tsc", "isc") else 0 if name[0] == "t" else 1
 
     def start(*names):
         for name in names:
-            copy(name).start()
+            group_name, copies, to = messages[name]
+            for src, dst in copies:
+                pltpu.make_async_remote_copy(
+                    src_ref=src,
+                    dst_ref=dst,
+                    send_sem=send_sem.at[sender(name)],
+                    recv_sem=recv_sem.at[groups[group_name][0]],
+                    device_id=to,
+                    device_id_type=pl.DeviceIdType.MESH,
+                ).start()
+
+    def all_of(ref, sem):
+        pltpu.make_async_copy(ref, ref, sem).wait()
 
     def got(*names):
         for name in names:
-            if name[0] == "s":
-                number, _, _, to = messages[name]
-                off = int(name[1:]) * 128 + (1 - core) * 64
-                there = ib.at[:, pl.ds(pl.multiple_of(off, 32), 64), :]
-                pltpu.make_async_remote_copy(
-                    src_ref=there,
-                    dst_ref=there,
-                    send_sem=send_sem.at[sender(name)],
-                    recv_sem=recv_sem.at[number],
-                    device_id=to,
-                    device_id_type=pl.DeviceIdType.MESH,
-                ).wait_recv()
-            else:
-                copy(name).wait_recv()
+            number, ref = groups[name]
+            all_of(ref, recv_sem.at[number])
 
     own_rows = pl.ds(pl.multiple_of(core * 64, 64), 64)
+    barrier = pltpu.get_barrier_semaphore()
+    near = (pair_x, next_x, pair_y, next_y)
+    for to in near + (up_z, dn_z, other_core, diag):
+        pl.semaphore_signal(barrier, inc=1, device_id=to, device_id_type=pl.DeviceIdType.MESH)
     loads = [
         (0, txt_l.at[0], tb.at[0, pl.ds(0, 2 * HALF), :]),
         (0, txt_r.at[0], tb.at[1, pl.ds(0, 2 * HALF), :]),
@@ -193,17 +219,11 @@
     for number, src, dst in loads:
         pltpu.make_async_copy(src, dst, local_sem.at[number]).start()
 
-    def all_of(ref, sem):
-        pltpu.make_async_copy(ref, ref, sem).wait()
-
-    barrier = pltpu.get_barrier_semaphore()
-    near = (pair_x, next_x, pair_y, next_y)
-    for to in near + (up_z, dn_z, other_core, diag):
-        pl.semaphore_signal(barrier, inc=1, device_id=to, device_id_type=pl.DeviceIdType.MESH)
+    pl.semaphore_wait(barrier, 8)
+    start("tsc", "isc", "ip", "t1p", "t2p", "io1l+", "io1l-", "io1r+", "io1r-")
     for number, ref in enumerate((tb.at[:, pl.ds(0, 2 * HALF), :], ib.at[:, own_rows, :], isc.at[0], tsc.at[0], ipr.at[0])):
         all_of(ref, local_sem.at[number])
-    pl.semaphore_wait(barrier, 8)
-    start("tsc", "isc", "ipr", "t1p", "t2p", "ip", "io1+", "io1-", "t1oP", "t2oP", "s0")
+    start("s0", "t1oNa", "t2oNa", "t2oNb", "t1oP", "t2oP")
 
     def tell(r):
         for to in near:
@@ -266,12 +286,12 @@
                 jnp.where(k < 6, lax.rem(k, 3), 3),
                 jnp.where(k < 12, k - 8, lax.div(k, 3)),
             ),
-            jnp.where(k < 26, jnp.where(k < 22, k - 18, 6), jnp.where(k < 28, k - 22, 7)),
+            jnp.where(k < 24, jnp.where(k < 22, k - 16, k - 22), lax.div(k, 4)),
         )
         chunk = jnp.where(
             k < 18,
             jnp.where(k < 8, jnp.where(k < 6, lax.div(k, 3), k - 6), jnp.where(k < 12, 2, lax.rem(k, 3))),
-            jnp.where(k < 26, jnp.where(k < 22, 3, k - 22), jnp.where(k < 28, 3, k - 28)),
+            jnp.where(k < 24, 3, lax.rem(k, 4)),
         )
         return block, chunk
 
@@ -345,79 +365,95 @@
             if piece // 2 in blocks:
                 row_copy(piece, which).start()
 
-    got("tsc", "isc", "ipr")
+    def sum_columns(pieces):
+        for piece in pieces:
+            px, py, half, same = source(piece)
+            line = jnp.sum(jnp.transpose(cs[pl.ds(piece * HALF, HALF), :]), axis=0, keepdims=True) * LN2
+            place = py if half == 0 else 4 + lax.div(px, 2) * 2 + lax.rem(py, 2)
+            col_part[0 if same else 1, place, :, 0:HALF] = line
+
+    got("scales")
     spread(1)
+    got("io1l")
+    start("io2l+", "io2l-")
     text_setup(1)
     image_setup(1)
-    got("io1+", "io1-")
-    start("s2", "s3")
+    got("io1r")
+    start("x11", "x1-1", "s2", "s3")
     got("ip")
-    start("iq1+", "iq1-", "io2+", "io2-", "s1", "t1oN", "t2oN")
+    start("iq1+", "iq1-", "io2r+", "io2r-", "s1", "t1oNb")
     told(0)
     tell(1)
-    got("t1p", "t2p")
+    got("tp")
     start("t1qP", "t2qP", "t1qN", "t2qN")
-    got("s0", "s1", "s2", "s3")
+    got("s0")
 
     def events(i):
         if i == 1:
-            got("iq1+", "iq1-")
-            start("iq2+", "iq2-", "s4", "s5")
-            got("t1oN", "t2oN")
+            got("iq1")
+            start("iq2+", "iq2-")
+            got("x1")
+            start("s4", "s5")
+            got("toN")
             start("t1o2B", "t2o2B")
-            got("t1oP", "t2oP")
+            got("io2")
+            start("x22", "x2-2", "s6", "s7", "io3+", "io3-")
+            got("toP")
             start("t1o2A", "t2o2A")
-            got("s4", "s5")
-        elif i == 2:
-            got("io2+", "io2-")
-            start("io3+", "io3-", "s6", "s7")
+            got("s2")
         elif i == 3:
-            got("s6", "s7")
+            got("s3")
             told(1)
             tell(2)
         elif i == 4:
-            got("t1qN", "t2qN")
+            got("iq2")
+            start("iq3+", "iq3-")
+            got("tqN")
             start("t1q2B", "t2q2B")
-            got("iq2+", "iq2-")
-            start("iq3+", "iq3-", "s8", "s9")
-            got("t1qP", "t2qP")
+            got("tqP")
             start("t1q2A", "t2q2A")
+        elif i == 5:
+            got("x2")
+            start("s8", "s9")
+            got("io3")
+            start("io4+", "io4-", "s10", "s11", "x33", "x3-3")
         elif i == 6:
-            got("s8", "s9")
+            got("s4")
         elif i == 7:
-            got("io3+", "io3-")
-            start("io4+", "io4-", "s10", "s11")
-            got("s10", "s11")
+            got("s5")
         elif i == 9:
-            got("t1o2A", "t1o2B", "t2o2A", "t2o2B", "t1q2A", "t1q2B", "t2q2A", "t2q2B")
+            got("iq3")
+            start("iq4+", "iq4-")
+            got("t2")
         elif i == 10:
-            got("iq3+", "iq3-")
-            start("iq4+", "iq4-", "s12", "s13")
+            got("io4")
+            start("x44", "s14")
         elif i == 11:
-            got("s12", "s13")
+            got("x3")
+            start("s12", "s13")
         elif i == 12:
-            got("io4+", "io4-")
-            start("s14")
+            told(2)
+            send_rows((0, 2, 3, 4, 5))
+            got("s6")
         elif i == 13:
-            told(2)
+            got("iq4", "x4")
+            start("s15")
         elif i == 14:
-            send_rows((0, 1, 2, 3, 4, 6))
-            got("iq4+", "iq4-")
-            start("s15")
-            got("s14", "s15")
+            send_rows((1,))
+            got("s7")
 
     dots(0, dl0, dr0)
     dots(1, dl1, dr1)
     scores(0, dl0, dr0)
 
-    @pl.loop(1, STEPS // 2)
+    @pl.loop(1, STEPS // 2 - 1)
     def _(i):
         for low, high in ((1, 4), (4, 10), (10, 15)):
 
             @pl.when((i >= low) & (i < high))
             def _(low=low, high=high):
                 for at in range(low, high):
-                    if at not in (5, 8):
+                    if at not in (2, 8):
 
                         @pl.when(i == at)
                         def _(at=at):
@@ -428,16 +464,18 @@
         dots(2 * i + 1, dl1, dr1)
         scores(2 * i, dl0, dr0)
 
+    dots(STEPS - 2, dl0, dr0)
+    scores(STEPS - 3, dl1, dr1)
+    send_rows((6,))
+    dots(STEPS - 1, dl1, dr1)
+    scores(STEPS - 2, dl0, dr0)
+    sum_columns(range(12))
     scores(STEPS - 1, dl1, dr1)
 
-    send_rows((5, 7))
+    send_rows((7,))
 
     mine = x * 4 + y
-    for piece in range(16):
-        px, py, half, same = source(piece)
-        line = jnp.sum(jnp.transpose(cs[pl.ds(piece * HALF, HALF), :]), axis=0, keepdims=True) * LN2
-        place = py if half == 0 else 4 + lax.div(px, 2) * 2 + lax.rem(py, 2)
-        col_part[0 if same else 1, place, :, 0:HALF] = line
+    sum_columns(range(12, 16))
 
     def col_copy(dx, dy):
         return pltpu.make_async_remote_copy(
@@ -461,24 +499,23 @@
         line = line + row_recv[number]
     row_out[...] = jnp.where(core == 0, line[:, :64], line[:, 64:])
     all_of(col_recv.at[pl.ds(0, 15)], col_sem.at[1])
-    for x_hi in range(2):
-        for yy in range(4):
-            at = [(2 * x_hi + a) * 4 + b for a in range(2) for b in range(4)]
-            col_out[pl.ds((x_hi * 4 + yy) * 2, 1), :] = functools.reduce(
-                lambda s, t: s + t, [col_recv[n, yy] for n in at]
-            )
-        for y_hi in range(2):
-            for y_low in range(2):
-                at = [a * 4 + 2 * y_hi + b for a in range(4) for b in range(2)]
-                col_out[pl.ds((x_hi * 4 + y_hi * 2 + y_low) * 2 + 1, 1), :] = functools.reduce(
-                    lambda s, t: s + t, [col_recv[n, 4 + x_hi * 2 + y_low] for n in at]
-                )
+    def summed(senders, place):
+        return functools.reduce(lambda s, t: s + t, [col_recv[n, place] for n in senders])[:, :HALF]
+
+    parts = []
+    for g in range(8):
+        x_hi, yy = g // 4, g % 4
+        parts.append(summed([(2 * x_hi + a) * 4 + b for a in range(2) for b in range(4)], yy))
+        parts.append(summed([a * 4 + yy // 2 * 2 + b for a in range(4) for b in range(2)], 4 + x_hi * 2 + yy % 2))
+    for q in range(4):
+        a, b, c, d = parts[4 * q : 4 * q + 4]
+        col_out[3 * q : 3 * q + 1, :] = jnp.concatenate([a, b[:, :32]], axis=1)
+        col_out[3 * q + 1 : 3 * q + 2, :] = jnp.concatenate([b[:, 32:], c[:, :64]], axis=1)
+        col_out[3 * q + 2 : 3 * q + 3, :] = jnp.concatenate([c[:, 64:], d], axis=1)
 
     all_of(tb.at[:, pl.ds(0, 14 * HALF), :], send_sem.at[0])
     all_of(ib.at[:, pl.ds(0, 31 * 64), :], send_sem.at[1])
-    all_of(tsc.at[0], send_sem.at[2])
-    all_of(isc.at[0], send_sem.at[3])
-    all_of(ipr.at[0], send_sem.at[4])
+    all_of(bc.at[0, 0, pl.ds(0, 72), :], send_sem.at[2])
     all_of(row_recv.at[pl.ds(0, 31)], row_sem.at[0])
     all_of(col_recv.at[pl.ds(0, 15)], col_sem.at[0])
 
@@ -499,7 +536,7 @@
     in_hbm = pl.BlockSpec(memory_space=pltpu.HBM)
     rows, cols = pl.pallas_call(
         functools.partial(kernel, (1.0 - offset) * LOG2E, (-1.0 - offset) * LOG2E),
-        out_shape=[jax.ShapeDtypeStruct((1, 64), F32), jax.ShapeDtypeStruct((16, 128), F32)],
+        out_shape=[jax.ShapeDtypeStruct((1, 64), F32), jax.ShapeDtypeStruct((12, 128), F32)],
         in_specs=[in_hbm] * 9,
         out_specs=[pl.BlockSpec(memory_space=vmem)] * 2,
         scratch_shapes=[
@@ -524,8 +561,8 @@
             vmem((2, 8, 1, 128), F32),
             vmem((16, 8, 1, 128), F32),
             dma((5,)),
-            dma((5,)),
-            dma((54,)),
+            dma((3,)),
+            dma((28,)),
             dma((2,)),
             dma((2,)),
             pltpu.SemaphoreType.REGULAR((3,)),
@@ -548,7 +585,7 @@
         text_scale_refer.reshape(12, 128),
         pair_index.reshape(16, 128),
     )
-    return rows.reshape(64), cols[:, :HALF].reshape(1536)
+    return rows.reshape(64), cols.reshape(1536)
 
 
 def solution(mesh):

time: 76.6 us -> 72.9 us (0.952)
  Pallas kernels: 73.9 us -> 70.4 us
    pallas_call x1, Pallas kernels: 73.9 us -> 70.4 us  [shards(): pl.pallas_call(functools.partial(kernel, (1.0 - offset) * LOG2E, (-1.0 -...]
    reshape x1 -> x0, local copies, waits for them, and re-layouts: 1.37 us -> none  [shards(): return (rows.reshape(64), cols[:, :HALF].reshape(1536))]
    unnamed x3 -> x4, local copies, waits for them, and re-layouts: 0.52 us -> 1.79 us
where the time goes in v3:
time: 72.9 us; the launch traced here: 72.8 us
  Pallas kernels  70.4 us (97%)
  local copies, waits for them, and re-layouts  1.79 us (2%)
    pallas_call x1, Pallas kernels, shards(): pl.pallas_call(functools.partial(kernel, (1.0 - offset) * LOG2E, (-1.0 -...  70.4 us
    unnamed x4, local copies, waits for them, and re-layouts  1.79 us

profile of v3, /device:TPU:1, one launch (start us, length us, event | category | flops | bytes accessed | tf_op | source)
XLA Modules:
  0.0 72.8 jit_solution(5918443071622993607)
XLA Ops:
  0.6 70.4 %gather_score.1 = (f32[1,64]{1,0:T(1,128)}, f32[12,128]{1,0:T(8,128)}) custom-call(bf16[64,1152]{1,0:T(8,128)(2,1)} %img_l.1, bf16[64,1152]{1,0:T(8,128)(2,1)} %img_r.1, bf16[1,192,1152]{2,1,0:T(8,128)(2,1)} %txt_l.1, bf16[1,192,1152]{2,1,0:T(8,128)(2,1)} %txt_r.1, f32[16,128]{1,0:T(8,128)} %bitcast.8, f32[16,128]{1,0:T(8,128)} %bitcast.9, ...), custom_call_target="tpu_custom_call" | custom-call | flops 14495514624 | bytes 2097152 | tf_op jit(solution)/shard_map/gather_score/pallas_call | solution.py:537
  71.0 0.0 copy-start
  71.0 1.2 %copy.13 = f32[64]{0:T(128)} copy(f32[64]{0:T(128)} %bitcast.13) | data formatting | bytes 512
  72.2 0.0 copy-done
  72.2 0.6 copy.14
Async XLA Ops:
  71.0 1.2 %copy-start = (f32[12,128]{1,0:T(8,128)S(1)}, f32[12,128]{1,0:T(8,128)}, u32[]{:S(2)}) copy-start(f32[12,128]{1,0:T(8,128)} %get-tuple-element.5) | copy-start | bytes 18436

commit v4 on v3

--- a/solution.py
+++ b/solution.py
@@ -21,6 +21,7 @@
 PIECE_Z = (0, 0, 1, -1, 1, -1, 2, -2, 2, -2, 3, -3, 3, -3, 4, 4)
 PIECE_LANE = (0, 1, 0, 0, 1, 1, 0, 0, 1, 1, 0, 0, 1, 1, 0, 1)
 STEPS = 32
+VMEM_GRANT = 56539217
 
 
 def wrap(value, size):
@@ -138,7 +139,8 @@
         for part, start_row, rows in (("a", 0, 32), ("b", 32, 64)):
             message(name + "oN" + part, "toN", [(text(first, start_row, rows), text(o + 1, start_row, rows))], to_n)
         message(name + "qP", "tqP", [(text(2 + first), text(o + 4))], to_p)
-        message(name + "qN", "tqN", [(text(2 + first), text(o + 5))], to_n)
+        for part, start_row in (("a", 0), ("b", 48)):
+            message(name + "qN" + part, "tqN", [(text(2 + first, start_row, 48), text(o + 5, start_row, 48))], to_n)
         message(name + "o2A", "t2", [(text(o, 0, 48), text(far, 0, 48))], to_n)
         message(name + "o2B", "t2", [(text(o + 1, 48, 48), text(far, 48, 48))], to_p)
         message(name + "q2A", "t2", [(text(o + 4, 0, 48), text(far + 2, 0, 48))], to_n)
@@ -385,7 +387,7 @@
     told(0)
     tell(1)
     got("tp")
-    start("t1qP", "t2qP", "t1qN", "t2qN")
+    start("t1qP", "t2qP", "t1qNa", "t2qNa")
     got("s0")
 
     def events(i):
@@ -397,7 +399,7 @@
             got("toN")
             start("t1o2B", "t2o2B")
             got("io2")
-            start("x22", "x2-2", "s6", "s7", "io3+", "io3-")
+            start("x22", "x2-2", "t1qNb", "t2qNb", "io3+", "io3-", "s6", "s7")
             got("toP")
             start("t1o2A", "t2o2A")
             got("s2")
@@ -408,13 +410,13 @@
         elif i == 4:
             got("iq2")
             start("iq3+", "iq3-")
+            got("x2")
+            start("s8", "s9")
             got("tqN")
             start("t1q2B", "t2q2B")
             got("tqP")
             start("t1q2A", "t2q2A")
         elif i == 5:
-            got("x2")
-            start("s8", "s9")
             got("io3")
             start("io4+", "io4-", "s10", "s11", "x33", "x3-3")
         elif i == 6:
@@ -568,7 +570,7 @@
             pltpu.SemaphoreType.REGULAR((3,)),
         ],
         compiler_params=pltpu.CompilerParams(
-            collective_id=0, has_side_effects=True, vmem_limit_bytes=60 * 2**20
+            collective_id=0, has_side_effects=True, vmem_limit_bytes=VMEM_GRANT
         ),
         cost_estimate=pl.CostEstimate(
             flops=4 * 2048 * 1536 * E, bytes_accessed=2**21, transcendentals=3 * 2048 * 1536

time: 72.9 us -> 71.7 us (0.984)
    unnamed x4 -> x2, local copies, waits for them, and re-layouts: 1.79 us -> 1.11 us
where the time goes in v4:
time: 71.7 us; the launch traced here: 71.6 us
  Pallas kernels  69.8 us (97%)
  local copies, waits for them, and re-layouts  1.11 us (2%)
    pallas_call x1, Pallas kernels, shards(): pl.pallas_call(functools.partial(kernel, (1.0 - offset) * LOG2E, (-1.0 -...  69.8 us

profile of v4, /device:TPU:1, one launch (start us, length us, event | category | flops | bytes accessed | tf_op | source)
XLA Modules:
  0.0 71.6 jit_solution(12953509399451588238)
XLA Ops:
  0.6 69.8 %gather_score.1 = (f32[1,64]{1,0:T(1,128)S(1)}, f32[12,128]{1,0:T(8,128)S(1)}) custom-call(bf16[64,1152]{1,0:T(8,128)(2,1)} %img_l.1, bf16[64,1152]{1,0:T(8,128)(2,1)} %img_r.1, bf16[1,192,1152]{2,1,0:T(8,128)(2,1)} %txt_l.1, bf16[1,192,1152]{2,1,0:T(8,128)(2,1)} %txt_r.1, f32[16,128]{1,0:T(8,128)} %bitcast.9, f32[16,128]{1,0:T(8,128)} %bitcast.10, ...), custom_call_target="tpu_custom_call" | custom-call | flops 14495514624 | bytes 2097152 | tf_op jit(solution)/shard_map/gather_score/pallas_call | solution.py:539
  70.5 0.5 copy.13
  71.0 0.6 copy.14

commit v5 on v4

--- a/solution.py
+++ b/solution.py
@@ -16,7 +16,7 @@
 E = 1152
 HALF = 96
 CHUNK = 4 * HALF
-SPLIT = {1: 1024, 2: 1024, 3: 1024, 4: 1024}
+SPLIT = {1: 1024, 2: 1024, 3: 1024, 4: 896}
 BLOCK = 256
 PIECE_Z = (0, 0, 1, -1, 1, -1, 2, -2, 2, -2, 3, -3, 3, -3, 4, 4)
 PIECE_LANE = (0, 1, 0, 0, 1, 1, 0, 0, 1, 1, 0, 0, 1, 1, 0, 1)
@@ -136,7 +136,7 @@
     for name, first, to_p, to_n in (("t1", 0, pair_y, next_y), ("t2", 1, pair_x, next_x)):
         o, far = 4 + 2 * first, 12 + first
         message(name + "oP", "toP", [(text(first), text(o))], to_p)
-        for part, start_row, rows in (("a", 0, 32), ("b", 32, 64)):
+        for part, start_row, rows in (("a", 0, 64), ("b", 64, 32)):
             message(name + "oN" + part, "toN", [(text(first, start_row, rows), text(o + 1, start_row, rows))], to_n)
         message(name + "qP", "tqP", [(text(2 + first), text(o + 4))], to_p)
         for part, start_row in (("a", 0), ("b", 48)):
@@ -372,12 +372,12 @@
             px, py, half, same = source(piece)
             line = jnp.sum(jnp.transpose(cs[pl.ds(piece * HALF, HALF), :]), axis=0, keepdims=True) * LN2
             place = py if half == 0 else 4 + lax.div(px, 2) * 2 + lax.rem(py, 2)
-            col_part[0 if same else 1, place, :, 0:HALF] = line
-
+            col_part[0 if same else 1, pl.ds(place, 1), 0:HALF] = line
+
+    got("io1l")
+    start("io2l+", "io2l-")
     got("scales")
     spread(1)
-    got("io1l")
-    start("io2l+", "io2l-")
     text_setup(1)
     image_setup(1)
     got("io1r")
@@ -501,14 +501,17 @@
         line = line + row_recv[number]
     row_out[...] = jnp.where(core == 0, line[:, :64], line[:, 64:])
     all_of(col_recv.at[pl.ds(0, 15)], col_sem.at[1])
-    def summed(senders, place):
-        return functools.reduce(lambda s, t: s + t, [col_recv[n, place] for n in senders])[:, :HALF]
-
+    def summed(senders):
+        return functools.reduce(lambda s, t: s + t, [col_recv[n] for n in senders])[:, :HALF]
+
+    over_x = [summed([(2 * x_hi + a) * 4 + b for a in range(2) for b in range(4)]) for x_hi in range(2)]
+    over_y = [summed([a * 4 + 2 * y_hi + b for a in range(4) for b in range(2)]) for y_hi in range(2)]
     parts = []
     for g in range(8):
         x_hi, yy = g // 4, g % 4
-        parts.append(summed([(2 * x_hi + a) * 4 + b for a in range(2) for b in range(4)], yy))
-        parts.append(summed([a * 4 + yy // 2 * 2 + b for a in range(4) for b in range(2)], 4 + x_hi * 2 + yy % 2))
+        at = 4 + x_hi * 2 + yy % 2
+        parts.append(over_x[x_hi][yy : yy + 1])
+        parts.append(over_y[yy // 2][at : at + 1])
     for q in range(4):
         a, b, c, d = parts[4 * q : 4 * q + 4]
         col_out[3 * q : 3 * q + 1, :] = jnp.concatenate([a, b[:, :32]], axis=1)
@@ -560,8 +563,8 @@
             vmem((CHUNK, BLOCK), F32),
             vmem((16, 1, 128), F32),
             vmem((32, 1, 128), F32),
-            vmem((2, 8, 1, 128), F32),
-            vmem((16, 8, 1, 128), F32),
+            vmem((2, 8, 128), F32),
+            vmem((16, 8, 128), F32),
             dma((5,)),
             dma((3,)),
             dma((28,)),

time: 71.7 us -> 71.6 us (level)
  no operation moved by 1% of the time
where the time goes in v5:
time: 71.6 us; the launch traced here: 71.5 us
  Pallas kernels  69.7 us (97%)
  local copies, waits for them, and re-layouts  1.11 us (2%)
    pallas_call x1, Pallas kernels, shards(): pl.pallas_call(functools.partial(kernel, (1.0 - offset) * LOG2E, (-1.0 -...  69.7 us

profile of v5, /device:TPU:1, one launch (start us, length us, event | category | flops | bytes accessed | tf_op | source)
XLA Modules:
  0.0 71.5 jit_solution(13582321343450733912)
XLA Ops:
  0.6 69.7 %gather_score.1 = (f32[1,64]{1,0:T(1,128)S(1)}, f32[12,128]{1,0:T(8,128)S(1)}) custom-call(bf16[64,1152]{1,0:T(8,128)(2,1)} %img_l.1, bf16[64,1152]{1,0:T(8,128)(2,1)} %img_r.1, bf16[1,192,1152]{2,1,0:T(8,128)(2,1)} %txt_l.1, bf16[1,192,1152]{2,1,0:T(8,128)(2,1)} %txt_r.1, f32[16,128]{1,0:T(8,128)} %bitcast.9, f32[16,128]{1,0:T(8,128)} %bitcast.10, ...), custom_call_target="tpu_custom_call" | custom-call | flops 14495514624 | bytes 2097152 | tf_op jit(solution)/shard_map/gather_score/pallas_call | solution.py:542
  70.4 0.5 copy.13
  70.9 0.6 copy.14

commit v6 on v5

--- a/solution.py
+++ b/solution.py
@@ -139,8 +139,9 @@
         for part, start_row, rows in (("a", 0, 64), ("b", 64, 32)):
             message(name + "oN" + part, "toN", [(text(first, start_row, rows), text(o + 1, start_row, rows))], to_n)
         message(name + "qP", "tqP", [(text(2 + first), text(o + 4))], to_p)
-        for part, start_row in (("a", 0), ("b", 48)):
-            message(name + "qN" + part, "tqN", [(text(2 + first, start_row, 48), text(o + 5, start_row, 48))], to_n)
+        for part, start_row, rows in (("a", 0, 64), ("b", 64, 32)):
+            piece = [(text(2 + first, start_row, rows), text(o + 5, start_row, rows))]
+            message(name + "qN" + part, "tqN", piece, to_n)
         message(name + "o2A", "t2", [(text(o, 0, 48), text(far, 0, 48))], to_n)
         message(name + "o2B", "t2", [(text(o + 1, 48, 48), text(far, 48, 48))], to_p)
         message(name + "q2A", "t2", [(text(o + 4, 0, 48), text(far + 2, 0, 48))], to_n)

time: 71.6 us -> 71.6 us (level)
  no operation moved by 1% of the time
where the time goes in v6:
time: 71.6 us; the launch traced here: 71.5 us
  Pallas kernels  69.7 us (97%)
  local copies, waits for them, and re-layouts  1.11 us (2%)
    pallas_call x1, Pallas kernels, shards(): pl.pallas_call(functools.partial(kernel, (1.0 - offset) * LOG2E, (-1.0 -...  69.7 us

profile of v6, /device:TPU:1, one launch (start us, length us, event | category | flops | bytes accessed | tf_op | source)
XLA Modules:
  0.0 71.5 jit_solution(12970062279542676795)
XLA Ops:
  0.6 69.7 %gather_score.1 = (f32[1,64]{1,0:T(1,128)S(1)}, f32[12,128]{1,0:T(8,128)S(1)}) custom-call(bf16[64,1152]{1,0:T(8,128)(2,1)} %img_l.1, bf16[64,1152]{1,0:T(8,128)(2,1)} %img_r.1, bf16[1,192,1152]{2,1,0:T(8,128)(2,1)} %txt_l.1, bf16[1,192,1152]{2,1,0:T(8,128)(2,1)} %txt_r.1, f32[16,128]{1,0:T(8,128)} %bitcast.9, f32[16,128]{1,0:T(8,128)} %bitcast.10, ...), custom_call_target="tpu_custom_call" | custom-call | flops 14495514624 | bytes 2097152 | tf_op jit(solution)/shard_map/gather_score/pallas_call | solution.py:543
  70.4 0.5 copy.13
  70.9 0.6 copy.14
